TPU v7x, 512 devices: a whole 4x8x8 slice. The times are simulated.
512 devices in a mesh: patch: 32 (over x_hi, z, core), freq: 16 (over y, x_lo).
Axes of the slice: x: 4 (x_hi: 2, x_lo: 2; x = x_hi * 2 + x_lo), y: 8, z: 8, core: 2. Of those that a mesh axis runs over, the one named last changes fastest.
Arguments:
- slip_rate: bfloat16 [2688, 4096], P('patch', 'freq'), may hold values from -6 to 6
- face_counts: int32 [32], P('patch'), may hold values from 12 to 84, as said below
- patch_ids: int32 [2688], P('patch'), may hold values from 0 to 1535, as said below
- moments: float32 [1536, 6], P('patch'), may hold values from -6 to 6
- green: bfloat16 [6, 2, 3, 496, 49152], P(None, None, None, 'freq', 'patch'), may hold values from -0.046875 to 0.046875
Outputs:
- seismograms: float32 [3, 496, 4096], P(None, 'freq', 'patch')
Inputs may be any that keep to these rules, and one draw needn't show every extreme that they name: The live slots of face i are its first face_counts[i] slots; the counts sum to 1536, one face has all 84 slots live and one has only 12. `patch_ids`: over the live slots of all faces every patch number appears exactly once; a dead slot holds an arbitrary patch number.
All inputs are finite; a program needn't handle non-finite values.
Results may differ from a plain program's by a relative error of at most 0.0029.
Values may be sent and summed in bfloat16 or wider, within the bound.
No kernel may reach another device: no remote copies, remote signals or barrier semaphores. Data moves between devices by JAX's collectives and lax.ppermute only.
A program may use at most 128 MiB of HBM per device.

v0:
```python
import math

import jax
import jax.numpy as jnp
from jax import lax
from jax.sharding import PartitionSpec as P

TIME_STEP_TOTAL = 4096
SPECTRAL_LINES = 32


def mode_indices():
    return 1 + jnp.arange(SPECTRAL_LINES, dtype=jnp.int32) * (
        TIME_STEP_TOTAL // (2 * SPECTRAL_LINES)
    )


def analysis_kernel(discrete_epochs):
    oscillation_argument = (
        discrete_epochs[:, None] * mode_indices()[None, :] % TIME_STEP_TOTAL
    ).astype(jnp.float32) * (2.0 * math.pi / TIME_STEP_TOTAL)
    layered_recordings = jnp.stack(
        [jnp.cos(oscillation_argument), -jnp.sin(oscillation_argument)], axis=-1
    ) * (1.0 / math.sqrt(TIME_STEP_TOTAL))
    return layered_recordings.reshape(discrete_epochs.shape[0], 2 * SPECTRAL_LINES)


def synthesis_kernel(discrete_epochs):
    oscillation_argument = (
        mode_indices()[:, None] * discrete_epochs[None, :] % TIME_STEP_TOTAL
    ).astype(jnp.float32) * (2.0 * math.pi / TIME_STEP_TOTAL)
    layered_recordings = jnp.stack(
        [jnp.cos(oscillation_argument), -jnp.sin(oscillation_argument)], axis=1
    ) * (1.0 / math.sqrt(SPECTRAL_LINES))
    return layered_recordings.reshape(2 * SPECTRAL_LINES, discrete_epochs.shape[0])


def mixing(spectrum, moments):
    real_part = spectrum[:, :, 0]
    imag_part = spectrum[:, :, 1]
    along_real = moments[:, :, None] * real_part[:, None, :]
    along_imag = moments[:, :, None] * imag_part[:, None, :]
    upper = jnp.stack([along_real, -along_imag])
    lower = jnp.stack([along_imag, along_real])
    return jnp.stack([upper, lower]).astype(jnp.bfloat16)


def local(slip_rate, face_counts, patch_ids, moments, green):
    capacity, dislocation_velocity_span = slip_rate.shape
    owned = moments.shape[0]
    stations_dev = green.shape[3]
    live_count = face_counts[0]
    alive_mask = jnp.arange(capacity, dtype=jnp.int32) < live_count
    discrete_epochs = lax.axis_index("freq") * dislocation_velocity_span + jnp.arange(
        dislocation_velocity_span, dtype=jnp.int32
    )
    recorded_waveform = jnp.where(alive_mask[:, None], slip_rate.astype(jnp.float32), 0.0)
    window_portion = jnp.dot(
        recorded_waveform, analysis_kernel(discrete_epochs), precision=lax.Precision.HIGHEST
    )
    owners = jnp.where(alive_mask, patch_ids, -1)
    numbers = jnp.arange(lax.axis_size("patch") * owned, dtype=jnp.int32)
    onehot = (numbers[:, None] == owners[None, :]).astype(jnp.float32)
    own_spectra = lax.psum_scatter(
        jnp.dot(onehot, window_portion, precision=lax.Precision.HIGHEST),
        "patch",
        scatter_dimension=0,
        tiled=True,
    )
    green_local = green.reshape(6, 2, 3, stations_dev, owned, SPECTRAL_LINES)
    spectra = lax.psum(own_spectra, "freq")
    weights = mixing(spectra.reshape(owned, SPECTRAL_LINES, 2), moments)
    partial_sums = jnp.einsum(
        "ogpkf,kgcspf->focs", weights, green_local, preferred_element_type=jnp.float32
    )
    station_spectra = lax.psum(partial_sums, "patch")
    time_spacing = TIME_STEP_TOTAL // lax.axis_size("patch")
    result_epochs = lax.axis_index("patch") * time_spacing + jnp.arange(
        time_spacing, dtype=jnp.int32
    )
    unrolled_records = station_spectra.reshape(2 * SPECTRAL_LINES, 3 * stations_dev)
    seismograms = jnp.dot(
        unrolled_records.T, synthesis_kernel(result_epochs), precision=lax.Precision.HIGHEST
    )
    return seismograms.reshape(3, stations_dev, time_spacing)


def solution(mesh):
    return jax.shard_map(
        local,
        mesh=mesh,
        in_specs=(
            P("patch", "freq"),
            P("patch"),
            P("patch"),
            P("patch", None),
            P(None, None, None, "freq", "patch"),
        ),
        out_specs=P(None, "freq", "patch"),
        check_vma=False,
    )
```

profile of v0, /device:TPU:4, one launch (start us, length us, event | category | flops | bytes accessed | tf_op | source)
XLA Modules:
  0.0 348.5 jit_solution(12360900624203463531)
XLA Ops:
  6.5 0.0 reduce-scatter.2.cloned.1.call-start
  6.5 0.2 fusion.16
  6.8 0.1 copy.32
  7.6 0.7 broadcast_select_fusion
  8.2 1.1 fusion.5
  9.3 1.4 fusion
  10.7 0.0 reduce-scatter.2.cloned.1.call-update
  10.7 17.6 %reshape.319 = bf16[6,2,3,31,48,32]{5,4,1,3,2,0:T(8,128)(2,1)} reshape(bf16[6,2,3,31,1536]{4,1,3,2,0:T(2,128)(2,1)} %param.9) | data formatting | bytes 6856704 | tf_op jit(solution)/shard_map/reshape | solution.py:70
  28.3 0.0 copy-start
  28.3 15.9 %copy.37 = bf16[6,2,3,31,48,32]{4,3,0,1,2,5:T(8,128)(2,1)} copy(bf16[6,2,3,31,48,32]{5,4,1,3,2,0:T(8,128)(2,1)} %reshape.319) | data formatting | bytes 6856704 | tf_op jit(solution)/shard_map/reshape | solution.py:70
  44.3 0.2 fusion.17
  44.5 94.5 %reduce-scatter.2.cloned.1.call-done = f32[48,64]{1,0:T(8,128)} async-done(((f32[1536,64]{1,0:T(8,128)}), f32[48,64]{1,0:T(8,128)}) %reduce-scatter.2.cloned.1.call-update) | async-done | bytes 12304 | tf_op jit(solution)/shard_map/reduce_scatter | solution.py:64
  139.0 0.8 copy.33
  139.8 63.1 %psum.14 = f32[48,32,2]{0,2,1:T(2,128)S(1)} all-reduce(f32[48,32,2]{0,2,1:T(2,128)S(1)} %bitcast.33), channel_id=1, replica_groups=mesh['patch'=32,'freq'=16] {'freq'}, use_global_device_ids=true, to_apply=%region_1.2 | all-reduce | flops 3072 | bytes 24576 | tf_op jit(solution)/shard_map/psum | solution.py:71
  203.0 0.0 copy-done
  203.1 0.2 copy.35
  203.2 0.2 copy.34
  203.4 8.6 %convolution_bitcast_fusion = f32[32,2,3,31]{3,1,2,0:T(2,128)S(1)} fusion(bf16[6,2,3,31,48,32]{4,3,0,1,2,5:T(8,128)(2,1)} %copy.37, bf16[1,2,48,6,32]{2,0,3,1,4:T(2,128)(2,1)S(1)} %copy.35, bf16[1,2,48,6,32]{2,0,3,1,4:T(2,128)(2,1)S(1)} %copy.34), kind=kOutput, calls=%fused_computation | convolution fusion | flops 7004160 | bytes 3525888 | tf_op jit(solution)/shard_map/ogpkf,kgcspf->focs/dot_general | solution.py:73
  212.1 0.1 reshape.315
  212.2 0.1 copy.39
  212.3 128.5 %psum.15 = f32[3,31,64]{2,1,0:T(8,128)S(1)} all-reduce(f32[3,31,64]{2,1,0:T(8,128)S(1)} %dot_general.20), channel_id=1, replica_groups=mesh['patch'=32,'freq'=16] {'patch'}, use_global_device_ids=true, to_apply=%region_2.3 | all-reduce | flops 5952 | bytes 47616 | tf_op jit(solution)/shard_map/psum | solution.py:76
  340.8 0.8 fusion.21
  (13 shorter events, 0.2 us)
Async XLA Ops:
  6.5 132.4 %reduce-scatter.2.cloned.1.call-start = ((), (), s32[]{:S(2)}) async-start(), calls=%async_computation.1 | async-start | bytes 811008 | tf_op jit(solution)/shard_map/reduce_scatter | solution.py:64
  28.3 174.6 %copy-start = (f32[48,6]{0,1:T(8,128)S(1)}, f32[48,6]{0,1:T(8,128)}, u32[]{:S(2)}) copy-start(f32[48,6]{0,1:T(8,128)} %param.8) | copy-start | bytes 3460
Sparse Core Ops, SparseCore 0:
  12.0 126.9 reduce-scatter.1
where the time goes:
time: 350 us; the launch traced here: 348 us
  blocking collectives  192 us (55%)
  waiting for transfers between devices  94.5 us (27%)
  local copies, waits for them, and re-layouts  35.1 us (10%)
  between operations  14.2 us (4%)
  matrix products  11.9 us (3%)
    psum x1, blocking collectives, local(): station_spectra = lax.psum(partial_sums, 'patch')  129 us
    reduce_scatter x1, waiting for transfers between devices, local(): lax.psum_scatter(jnp.dot(onehot, window_portion, precision=lax.Precision....  94.5 us
    psum x1, blocking collectives, local(): spectra = lax.psum(own_spectra, 'freq')  63.1 us
    reshape x2, local copies, waits for them, and re-layouts, local(): green_local = green.reshape(6, 2, 3, stations_dev, owned, SPECTRAL_LINES)  33.6 us
    dot_general x1, matrix products, local(): jnp.einsum('ogpkf,kgcspf->focs', weights, green_local, preferred_element_...  8.64 us
  transfers between devices with their start and end apart: 1, of which 1 were waited for; matrix products, arithmetic and copies ran while one was open for 10% of the time, Pallas kernels for 0%

commit v1 on v0

v1 whole, which is shorter than its diff:
```python
import functools
import math

import jax
import jax.numpy as jnp
import numpy as np
from jax import lax
from jax.experimental import pallas as pl
from jax.experimental.pallas import tpu as pltpu
from jax.sharding import PartitionSpec as P

T = 4096
BINS = 32
FACES = 32
WINDOWS = 16
CAP = 84
OWN = 48
STA_DEV = 31
HOLD = 96
ID_ROW = 88

CORE_PAIRS = [[2 * d, 2 * d + 1] for d in range(16)]
SAME_CORE = [[2 * d + c for d in range(16)] for c in range(2)]

f32 = jnp.float32
bf16 = jnp.bfloat16


def split2(x):
    hi = x.astype(bf16)
    return hi, (x - hi.astype(f32)).astype(bf16)


def np_split2(x):
    hi = x.astype(np.float32).astype(jnp.bfloat16)
    lo = (x - hi.astype(np.float64)).astype(np.float32).astype(jnp.bfloat16)
    return hi, lo


def angles(samples):
    k = 1 + np.arange(BINS) * (T // (2 * BINS))
    return 2.0 * np.pi * ((np.arange(samples)[:, None] * k[None, :]) % T) / T


def analysis_table():
    ang = angles(T // WINDOWS)
    c, s = np.cos(ang) / math.sqrt(T), np.sin(ang) / math.sqrt(T)
    straight = np.concatenate([c, -s, c, -s], axis=1)
    turned = np.concatenate([-s, -c, -s, -c], axis=1)
    s_hi, s_lo = np_split2(straight)
    t_hi, t_lo = np_split2(turned)
    return np.concatenate([s_hi, t_hi, s_lo, t_lo], axis=1)


def synthesis_table():
    ang = angles(T // FACES).T
    c, s = np.cos(ang) / math.sqrt(BINS), -np.sin(ang) / math.sqrt(BINS)
    z = np.zeros_like(c)
    first = np.concatenate([c, z, s, z], axis=0)
    second = np.concatenate([z, c, z, s], axis=0)
    hi, lo = np_split2(np.concatenate([first, second], axis=1))
    return np.concatenate([hi, hi, lo], axis=0)


def turns(n):
    a = 2.0 * np.pi * np.arange(n) / n
    return np.concatenate([np.cos(a), np.sin(a)]).astype(np.float32)


def lanes(shape):
    return lax.broadcasted_iota(jnp.int32, shape, len(shape) - 1)


def rows(shape):
    return lax.broadcasted_iota(jnp.int32, shape, len(shape) - 2)


def window_kernel(count, turn, slip, ids, table, out):
    q = lax.axis_index("freq")
    r = jnp.dot(slip[...], table[...], preferred_element_type=f32)
    x = turn[q] * (r[:, :128] + r[:, 256:384]) + turn[q + WINDOWS] * (
        r[:, 128:256] + r[:, 384:]
    )
    out[0:CAP, :] = jnp.where(rows((CAP, 128)) < count[0], x, 0.0)
    out[ID_ROW:HOLD, :] = jnp.full((HOLD - ID_ROW, 128), -1.0, f32)
    out[CAP:ID_ROW, :] = jnp.zeros((ID_ROW - CAP, 128), f32)
    live = lanes((1, CAP)) < count[0]
    out[ID_ROW : ID_ROW + 1, 0:CAP] = jnp.where(live, ids[...].astype(f32), -1.0)


def route_kernel(held, out):
    core = lax.rem(lax.axis_index("patch"), 2).astype(f32)
    n = 16 * 24
    r = rows((n, 128))
    d = lax.shift_right_logical(r * 2731, 16)
    j = lax.shift_right_logical(r - 24 * d, 1)
    base = (96 * d + 4 * j).astype(f32)
    block = lax.shift_right_logical(lanes((HOLD, 256)), 5) % 4
    odd = lax.rem(lax.shift_right_logical(lanes((HOLD, 128)), 5), 2) == 1
    left, right_hi, right_lo = [], [], []
    for k in range(2):
        x = held[k]
        re = jnp.where(odd, pltpu.roll(x, 32, 1), x)
        im = jnp.where(odd, x, pltpu.roll(x, 96, 1))
        hi, lo = split2(jnp.concatenate([re, im], axis=1))
        hi, lo = hi.astype(f32), lo.astype(f32)
        owner = held[k, ID_ROW : ID_ROW + 1, :]
        ahead = owner - base - 48.0 * core
        pad = jnp.zeros((128 - HOLD, 256), f32)
        for b in range(4):
            left.append(jnp.where(ahead == float(b), 1.0, 0.0))
            right_hi.append(jnp.where(block == b, hi, 0.0))
            right_hi.append(pad)
            right_lo.append(jnp.where(block == b, lo, 0.0))
            right_lo.append(pad)
    lhs = jnp.concatenate(left, axis=1).astype(bf16)
    rhs_hi = jnp.concatenate(right_hi, axis=0).astype(bf16)
    rhs_lo = jnp.concatenate(right_lo, axis=0).astype(bf16)
    got = jnp.dot(lhs, rhs_hi, preferred_element_type=f32) + jnp.dot(
        lhs, rhs_lo, preferred_element_type=f32
    )
    even = lax.rem(r, 2) == 0
    out[...] = jnp.where(even, got[:, :128], got[:, 128:]).reshape(16, 24, 128)


def spread_kernel(got, out):
    total = jnp.sum(got[...], axis=0)
    out[...] = jnp.broadcast_to(total[None], out.shape)


def sublane_sums(parts):
    sub = rows((8, 128))
    dist = 4
    while dist >= 1:
        low = (lax.shift_right_logical(sub, dist.bit_length() - 1) % 2) == 0
        parts = [
            jnp.where(low, a, b) + pltpu.roll(jnp.where(low, b, a), dist, 0)
            if dist == 4
            else jnp.where(low, a, b)
            + jnp.where(
                low, pltpu.roll(a, 8 - dist, 0), pltpu.roll(b, dist, 0)
            )
            for a, b in zip(parts[: len(parts) // 2], parts[len(parts) // 2 :])
        ]
        dist //= 2
    return parts[0]


def green_kernel(green, moments, got, out):
    s = jnp.sum(got[...], axis=0)
    even = lax.rem(rows((24, 128)), 2) == 0
    swapped = jnp.where(even, pltpu.roll(s, 23, 0), pltpu.roll(s, 1, 0))
    for_re = jnp.where(even, s, -s)
    for_im = swapped
    pick = lax.shift_right_logical(rows((24, OWN)), 1) == lax.shift_right_logical(
        lanes((24, OWN)), 2
    )
    spread = jnp.where(
        lax.rem(rows((OWN, 128)), 4) == lax.shift_right_logical(lanes((OWN, 128)), 5),
        1.0,
        0.0,
    ).astype(bf16)
    m_rows = jnp.concatenate(
        [jnp.where(pick, moments[m : m + 1, :], 0.0) for m in range(6)], axis=0
    )
    m_hi, m_lo = split2(m_rows)
    m_all = jnp.dot(m_hi, spread, preferred_element_type=f32) + jnp.dot(
        m_lo, spread, preferred_element_type=f32
    )
    lane = lanes((8, 128))
    half = lane < 64
    block_even = lax.rem(lax.shift_right_logical(lane, 5), 2) == 0
    stride = 3 * STA_DEV * 24
    folded = []
    for c in range(3):
        for s0 in range(0, 32, 8):
            n = min(8, STA_DEV - s0)
            acc = None
            for m in range(6):
                start = m * stride + (c * STA_DEV + s0) * 24
                stop = start + n * 24
                a, z = start // 16 * 16, -(-stop // 16) * 16
                g = green[a:z, :].astype(f32)[start - a : stop - a]
                w = m_all[24 * m : 24 * m + 24]
                term = g.reshape(n, 24, 128) * w[None]
                acc = term if acc is None else acc + term
            sums = []
            for weight in (for_re, for_im):
                p = (acc * weight[None]).reshape(n, 3, 8, 128)
                p = p[:, 0] + p[:, 1] + p[:, 2]
                parts = [p[i] for i in range(n)] + [jnp.zeros((8, 128), f32)] * (8 - n)
                sums.append(sublane_sums(parts))
            a, b = sums
            folded.append(
                jnp.where(half, a, b) + pltpu.roll(jnp.where(half, b, a), 64, 1)
            )
    for i in range(6):
        a, b = folded[i], folded[i + 6]
        w = jnp.where(block_even, a, b)
        z = jnp.where(block_even, pltpu.roll(a, 96, 1), pltpu.roll(b, 32, 1))
        out[8 * i : 8 * i + 8, :] = w + z


def series_kernel(turn, got, table, out):
    p = lax.axis_index("patch")
    x = jnp.sum(got[...], axis=0)
    other = pltpu.roll(x, 64, 1)
    real = lanes((48, 128)) < 64
    x = turn[p] * x + turn[p + FACES] * jnp.where(real, -other, other)
    hi, lo = split2(x)
    lhs = jnp.concatenate([hi, lo, hi], axis=1)
    y = jnp.dot(lhs, table[...], preferred_element_type=f32)
    y = jnp.concatenate([y[:, :128], y[:, 128:]], axis=0)
    for c in range(3):
        out[c] = y[32 * c : 32 * c + STA_DEV]


VMEM = pl.BlockSpec(memory_space=pltpu.VMEM)
SMEM = pl.BlockSpec(memory_space=pltpu.SMEM)


def call(kernel, shape, specs, *args, dtype=f32):
    return pl.pallas_call(
        kernel,
        out_shape=jax.ShapeDtypeStruct(shape, dtype),
        in_specs=specs,
        out_specs=VMEM,
        compiler_params=pltpu.CompilerParams(vmem_limit_bytes=32 * 1024 * 1024),
    )(*args)


def local(slip_rate, face_counts, patch_ids, moments, green):
    held = call(
        window_kernel,
        (HOLD, 128),
        [SMEM, SMEM, VMEM, VMEM, VMEM],
        face_counts,
        jnp.asarray(turns(WINDOWS)),
        slip_rate,
        patch_ids.reshape(1, CAP),
        jnp.asarray(analysis_table()),
    )
    held = lax.all_gather(held, "patch", axis_index_groups=CORE_PAIRS)
    blocks = call(route_kernel, (16, 24, 128), [VMEM], held)
    blocks = lax.all_to_all(
        blocks, "patch", 0, 0, axis_index_groups=SAME_CORE, tiled=True
    )
    copies = call(spread_kernel, (16, 24, 128), [VMEM], blocks)
    copies = lax.all_to_all(copies, "freq", 0, 0, tiled=True)
    tiles = green.transpose(0, 2, 3, 1, 4).reshape(6, 3, STA_DEV, 2, 12, 128)
    tiles = tiles.transpose(0, 1, 2, 4, 3, 5).reshape(6 * 3 * STA_DEV * 24, 128)
    partial = call(
        green_kernel, (48, 128), [VMEM, VMEM, VMEM], tiles, moments.T, copies
    )
    pair = lax.all_gather(partial, "patch", axis_index_groups=CORE_PAIRS)
    copies = call(spread_kernel, (16, 48, 128), [VMEM], pair)
    copies = lax.all_to_all(
        copies, "patch", 0, 0, axis_index_groups=SAME_CORE, tiled=True
    )
    return call(
        series_kernel,
        (3, STA_DEV, 128),
        [SMEM, VMEM, VMEM],
        jnp.asarray(turns(FACES)),
        copies,
        jnp.asarray(synthesis_table()),
    )


def solution(mesh):
    return jax.shard_map(
        local,
        mesh=mesh,
        in_specs=(
            P("patch", "freq"),
            P("patch"),
            P("patch"),
            P("patch", None),
            P(None, None, None, "freq", "patch"),
        ),
        out_specs=P(None, "freq", "patch"),
        check_vma=False,
    )
```

time: 350 us -> 77 us (0.22)
  the two profiles are of different devices: /device:TPU:4 before, /device:TPU:8 now
where the time goes in v1:
time: 77 us; the launch traced here: 76.6 us
  blocking collectives  46.5 us (60%)
  local copies, waits for them, and re-layouts  16.1 us (21%)
  starting transfers between devices  7.59 us (10%)
  Pallas kernels  5.6 us (7%)
    all_to_all x1, blocking collectives, local(): lax.all_to_all(blocks, 'patch', 0, 0, axis_index_groups=SAME_CORE, tiled=...  23.2 us
    all_to_all x1, blocking collectives, local(): lax.all_to_all(copies, 'patch', 0, 0, axis_index_groups=SAME_CORE, tiled=...  19.6 us
    all_to_all x1, starting transfers between devices, local(): copies = lax.all_to_all(copies, 'freq', 0, 0, tiled=True)  7.59 us
    transpose x1, local copies, waits for them, and re-layouts, local(): tiles = tiles.transpose(0, 1, 2, 4, 3, 5).reshape(6 * 3 * STA_DEV * 24, 128)  5.83 us
    pallas_call x6, Pallas kernels, call(): pl.pallas_call(kernel, out_shape=jax.ShapeDtypeStruct(shape, dtype), in_s...  5.6 us
    reshape x1, local copies, waits for them, and re-layouts, local(): tiles = green.transpose(0, 2, 3, 1, 4).reshape(6, 3, STA_DEV, 2, 12, 128)  4.56 us
    unnamed x14, local copies, waits for them, and re-layouts  3.06 us
    transpose x1, local copies, waits for them, and re-layouts, local(): tiles = green.transpose(0, 2, 3, 1, 4).reshape(6, 3, STA_DEV, 2, 12, 128)  2.67 us
  transfers between devices with their start and end apart: 1, of which 0 were waited for; matrix products, arithmetic and copies ran while one was open for 17% of the time, Pallas kernels for 0%

profile of v1, /device:TPU:8, one launch (start us, length us, event | category | flops | bytes accessed | tf_op | source)
XLA Modules:
  0.0 76.6 jit_solution(10897169635410684013)
XLA Ops:
  0.7 0.0 copy-start
  0.7 0.9 %copy-done = bf16[256,512]{1,0:T(8,128)(2,1)S(1)} copy-done((bf16[256,512]{1,0:T(8,128)(2,1)S(1)}, bf16[256,512]{1,0:T(8,128)(2,1)}, u32[]{:S(2)}) %copy-start) | copy-done | bytes 262168
  1.6 0.0 copy-start.2
  1.6 0.8 %copy-done.2 = bf16[84,256]{1,0:T(8,128)(2,1)S(1)} copy-done((bf16[84,256]{1,0:T(8,128)(2,1)S(1)}, bf16[84,256]{1,0:T(8,128)(2,1)}, u32[]{:S(2)}) %copy-start.2) | copy-done | bytes 43032
  2.4 0.0 copy-start.4
  2.4 0.7 copy-done.4
  3.1 0.0 copy-start.5
  3.1 0.7 copy-done.5
  3.7 0.7 shard_map.91
  4.4 1.9 %all-gather = f32[192,128]{1,0:T(8,128)S(1)} all-gather(f32[96,128]{1,0:T(8,128)S(1)} %shard_map.91), channel_id=2, replica_groups={{0,16},{32,48},{64,80},{96,112},{128,144},{160,176},{192,208},{224,240}..., dimensions={0}, use_global_device_ids=true | all-gather | bytes 147456 | tf_op jit(solution)/shard_map/all_gather | solution.py:243
  6.3 0.7 shard_map.92
  7.0 23.2 %all_to_all.15.got = f32[16,24,128]{2,1,0:T(8,128)S(1)} all-to-all(f32[16,24,128]{2,1,0:T(8,128)S(1)} %shard_map.92), channel_id=1, replica_groups={{0,32,64,96,128,160,192,224,256,288,320,352,384,416,448,480},{16,48,80,..., dimensions={0} | all-to-all | bytes 393216 | tf_op jit(solution)/shard_map/all_to_all | solution.py:245
  30.2 0.7 shard_map.93
  30.9 7.6 %all-to-all-start.1 = ((f32[16,24,128]{2,1,0:T(8,128)}), f32[16,24,128]{2,1,0:T(8,128)}, u32[]{:S(2)}, u32[]{:S(2)}) async-start(f32[16,24,128]{2,1,0:T(8,128)} %shard_map.93), calls=%async_computation.1 | async-start | bytes 393216 | tf_op jit(solution)/shard_map/all_to_all | solution.py:249
  38.5 2.7 %copy.11 = bf16[6,3,31,2,1536]{4,2,3,1,0:T(8,128)(2,1)S(1)} copy(bf16[6,3,31,2,1536]{4,3,2,1,0:T(2,128)(2,1)} %bitcast.15) | data formatting | bytes 6856704 | tf_op jit(solution)/shard_map/transpose | solution.py:250
  41.2 4.6 %reshape.9 = bf16[6,3,31,2,12,128]{5,4,2,3,1,0:T(8,128)(2,1)} reshape(bf16[6,3,31,2,1536]{4,2,3,1,0:T(8,128)(2,1)S(1)} %copy.11) | data formatting | bytes 6856704 | tf_op jit(solution)/shard_map/reshape | solution.py:250
  45.7 0.0 copy-start.3
  45.7 5.8 %copy.12 = bf16[6,3,31,12,2,128]{5,4,3,2,1,0:T(2,128)(2,1)S(1)} copy(bf16[6,3,31,12,2,128]{5,3,2,4,1,0:T(8,128)(2,1)} %bitcast.14) | data formatting | bytes 6856704 | tf_op jit(solution)/shard_map/transpose | solution.py:251
  51.6 0.0 copy-start.6
  51.6 0.0 all-to-all-done.1.got
  51.6 0.0 copy-start.1
  51.6 0.0 copy-done.3
  51.6 2.1 %shard_map.94 = f32[48,128]{1,0:T(8,128)S(1)} custom-call(bf16[13392,128]{1,0:T(8,128)(2,1)S(1)} %bitcast.9, f32[6,48]{1,0:T(8,128)S(1)} %bitcast.12, f32[16,24,128]{2,1,0:T(8,128)} %all-to-all-done.1.got), custom_call_target="tpu_custom_call" | custom-call | tf_op jit(solution)/shard_map/pallas_call | solution.py:223
  53.7 1.8 %all-gather.1 = f32[96,128]{1,0:T(8,128)S(1)} all-gather(f32[48,128]{1,0:T(8,128)S(1)} %shard_map.94), channel_id=3, replica_groups={{0,16},{32,48},{64,80},{96,112},{128,144},{160,176},{192,208},{224,240}..., dimensions={0}, use_global_device_ids=true | all-gather | bytes 73728 | tf_op jit(solution)/shard_map/all_gather | solution.py:255
  55.6 19.6 %all_to_all.16.got = f32[16,48,128]{2,1,0:T(8,128)S(1)} all-to-all(f32[16,48,128]{2,1,0:T(8,128)S(1)} %shard_map.95), channel_id=1, replica_groups={{0,32,64,96,128,160,192,224,256,288,320,352,384,416,448,480},{16,48,80,..., dimensions={0} | all-to-all | bytes 786432 | tf_op jit(solution)/shard_map/all_to_all | solution.py:257
  75.2 0.0 copy-done.6
  75.2 0.0 copy-done.1
  75.2 1.4 %shard_map.96 = f32[3,31,128]{2,1,0:T(8,128)} custom-call(f32[64]{0:T(128)S(1)} %copy-done.6, f32[16,48,128]{2,1,0:T(8,128)S(1)} %all_to_all.16.got, bf16[384,256]{1,0:T(8,128)(2,1)S(1)} %copy-done.1), custom_call_target="tpu_custom_call" | custom-call | tf_op jit(solution)/shard_map/pallas_call | solution.py:223
  (1 shorter events, 0.0 us)
Async XLA Ops:
  0.7 1.0 %copy-start = (bf16[256,512]{1,0:T(8,128)(2,1)S(1)}, bf16[256,512]{1,0:T(8,128)(2,1)}, u32[]{:S(2)}) copy-start(bf16[256,512]{1,0:T(8,128)(2,1)} %constant.9.clone.table) | copy-start | bytes 786436
  1.6 0.8 %copy-start.2 = (bf16[84,256]{1,0:T(8,128)(2,1)S(1)}, bf16[84,256]{1,0:T(8,128)(2,1)}, u32[]{:S(2)}) copy-start(bf16[84,256]{1,0:T(8,128)(2,1)} %slip.1) | copy-start | bytes 129028
  2.4 0.7 copy-start.4
  3.1 0.7 copy-start.5
  30.9 20.7 %all-to-all-start.1 = ((f32[16,24,128]{2,1,0:T(8,128)}), f32[16,24,128]{2,1,0:T(8,128)}, u32[]{:S(2)}, u32[]{:S(2)}) async-start(f32[16,24,128]{2,1,0:T(8,128)} %shard_map.93), calls=%async_computation.1 | async-start | bytes 393216 | tf_op jit(solution)/shard_map/all_to_all | solution.py:249
  45.7 5.9 %copy-start.3 = (f32[48,6]{0,1:T(8,128)S(1)}, f32[48,6]{0,1:T(8,128)}, u32[]{:S(2)}) copy-start(f32[48,6]{0,1:T(8,128)} %param.12) | copy-start | bytes 3460
  51.6 23.6 %copy-start.6 = (f32[64]{0:T(128)S(1)}, f32[64]{0:T(128)}, u32[]{:S(2)}) copy-start(f32[64]{0:T(128)} %constant.10.clone.turn) | copy-start | bytes 772
  51.6 23.6 %copy-start.1 = (bf16[384,256]{1,0:T(8,128)(2,1)S(1)}, bf16[384,256]{1,0:T(8,128)(2,1)}, u32[]{:S(2)}) copy-start(bf16[384,256]{1,0:T(8,128)(2,1)} %constant.11.clone.table) | copy-start | bytes 589828

commit v2 on v1

--- a/solution.py
+++ b/solution.py
@@ -31,25 +31,18 @@
     return hi, (x - hi.astype(f32)).astype(bf16)
 
 
-def np_split2(x):
-    hi = x.astype(np.float32).astype(jnp.bfloat16)
-    lo = (x - hi.astype(np.float64)).astype(np.float32).astype(jnp.bfloat16)
-    return hi, lo
-
-
 def angles(samples):
     k = 1 + np.arange(BINS) * (T // (2 * BINS))
     return 2.0 * np.pi * ((np.arange(samples)[:, None] * k[None, :]) % T) / T
 
 
 def analysis_table():
-    ang = angles(T // WINDOWS)
-    c, s = np.cos(ang) / math.sqrt(T), np.sin(ang) / math.sqrt(T)
-    straight = np.concatenate([c, -s, c, -s], axis=1)
-    turned = np.concatenate([-s, -c, -s, -c], axis=1)
-    s_hi, s_lo = np_split2(straight)
-    t_hi, t_lo = np_split2(turned)
-    return np.concatenate([s_hi, t_hi, s_lo, t_lo], axis=1)
+    t = np.arange(T)[:, None]
+    k = 1 + np.arange(BINS) * (T // (2 * BINS))
+    ang = 2.0 * np.pi * ((t * k) % T) / T
+    c, s = np.cos(ang) / math.sqrt(T), -np.sin(ang) / math.sqrt(T)
+    table = np.concatenate([c, s, c, s], axis=1).astype(np.float32)
+    return table.reshape(WINDOWS, T // WINDOWS, 128)
 
 
 def synthesis_table():
@@ -58,8 +51,7 @@
     z = np.zeros_like(c)
     first = np.concatenate([c, z, s, z], axis=0)
     second = np.concatenate([z, c, z, s], axis=0)
-    hi, lo = np_split2(np.concatenate([first, second], axis=1))
-    return np.concatenate([hi, hi, lo], axis=0)
+    return np.concatenate([first, second], axis=1).astype(np.float32)
 
 
 def turns(n):
@@ -75,12 +67,21 @@
     return lax.broadcasted_iota(jnp.int32, shape, len(shape) - 2)
 
 
-def window_kernel(count, turn, slip, ids, table, out):
+def window_kernel(count_hbm, slip_hbm, ids_hbm, table_hbm, out, count, slip, ids, table, sems):
     q = lax.axis_index("freq")
-    r = jnp.dot(slip[...], table[...], preferred_element_type=f32)
-    x = turn[q] * (r[:, :128] + r[:, 256:384]) + turn[q + WINDOWS] * (
-        r[:, 128:256] + r[:, 384:]
-    )
+    copies = [
+        pltpu.make_async_copy(count_hbm, count, sems.at[0]),
+        pltpu.make_async_copy(ids_hbm, ids, sems.at[1]),
+        pltpu.make_async_copy(slip_hbm, slip, sems.at[2]),
+        pltpu.make_async_copy(table_hbm.at[q], table, sems.at[3]),
+    ]
+    for copy in copies:
+        copy.start()
+    for copy in copies:
+        copy.wait()
+    both = jnp.concatenate(split2(table[...]), axis=1)
+    r = jnp.dot(slip[...], both, preferred_element_type=f32)
+    x = r[:, :128] + r[:, 128:]
     out[0:CAP, :] = jnp.where(rows((CAP, 128)) < count[0], x, 0.0)
     out[ID_ROW:HOLD, :] = jnp.full((HOLD - ID_ROW, 128), -1.0, f32)
     out[CAP:ID_ROW, :] = jnp.zeros((ID_ROW - CAP, 128), f32)
@@ -146,44 +147,44 @@
     return parts[0]
 
 
-def green_kernel(green, moments, got, out):
-    s = jnp.sum(got[...], axis=0)
-    even = lax.rem(rows((24, 128)), 2) == 0
-    swapped = jnp.where(even, pltpu.roll(s, 23, 0), pltpu.roll(s, 1, 0))
-    for_re = jnp.where(even, s, -s)
-    for_im = swapped
-    pick = lax.shift_right_logical(rows((24, OWN)), 1) == lax.shift_right_logical(
-        lanes((24, OWN)), 2
-    )
+def moment_kernel(green, moments, out, weights):
     spread = jnp.where(
-        lax.rem(rows((OWN, 128)), 4) == lax.shift_right_logical(lanes((OWN, 128)), 5),
+        rows((OWN, OWN * BINS)) == lax.shift_right_logical(lanes((OWN, OWN * BINS)), 5),
         1.0,
         0.0,
     ).astype(bf16)
-    m_rows = jnp.concatenate(
-        [jnp.where(pick, moments[m : m + 1, :], 0.0) for m in range(6)], axis=0
-    )
-    m_hi, m_lo = split2(m_rows)
-    m_all = jnp.dot(m_hi, spread, preferred_element_type=f32) + jnp.dot(
-        m_lo, spread, preferred_element_type=f32
-    )
+    hi, lo = split2(moments[...])
+    w = jnp.dot(hi, spread, preferred_element_type=f32) + jnp.dot(
+        lo, spread, preferred_element_type=f32
+    )
+    for m in range(6):
+        weights[m] = jnp.broadcast_to(w[m : m + 1], (2, OWN * BINS))
+    n_rows = 3 * STA_DEV
+    for i in range(0, n_rows, 8):
+        n = min(8, n_rows - i)
+        acc = None
+        for m in range(6):
+            at = m * n_rows + i
+            term = green[at : at + n].astype(f32) * weights[m][None]
+            acc = term if acc is None else acc + term
+        for j in range(12):
+            out[i : i + n, 2 * j : 2 * j + 2, :] = acc[:, :, 128 * j : 128 * j + 128]
+
+
+def patch_kernel(tiles, got, out):
+    s = jnp.sum(got[...], axis=0)
+    even = lax.rem(rows((24, 128)), 2) == 0
+    for_re = jnp.where(even, s, -s)
+    for_im = jnp.where(even, pltpu.roll(s, 23, 0), pltpu.roll(s, 1, 0))
     lane = lanes((8, 128))
     half = lane < 64
     block_even = lax.rem(lax.shift_right_logical(lane, 5), 2) == 0
-    stride = 3 * STA_DEV * 24
     folded = []
     for c in range(3):
         for s0 in range(0, 32, 8):
             n = min(8, STA_DEV - s0)
-            acc = None
-            for m in range(6):
-                start = m * stride + (c * STA_DEV + s0) * 24
-                stop = start + n * 24
-                a, z = start // 16 * 16, -(-stop // 16) * 16
-                g = green[a:z, :].astype(f32)[start - a : stop - a]
-                w = m_all[24 * m : 24 * m + 24]
-                term = g.reshape(n, 24, 128) * w[None]
-                acc = term if acc is None else acc + term
+            at = c * STA_DEV + s0
+            acc = tiles[at : at + n]
             sums = []
             for weight in (for_re, for_im):
                 p = (acc * weight[None]).reshape(n, 3, 8, 128)
@@ -201,15 +202,22 @@
         out[8 * i : 8 * i + 8, :] = w + z
 
 
+def spread_half_kernel(got, out):
+    total = jnp.sum(got[...], axis=0).astype(bf16)
+    out[...] = jnp.broadcast_to(total[None], out.shape)
+
+
 def series_kernel(turn, got, table, out):
     p = lax.axis_index("patch")
-    x = jnp.sum(got[...], axis=0)
+    x = jnp.sum(got[...].astype(f32), axis=0)
     other = pltpu.roll(x, 64, 1)
     real = lanes((48, 128)) < 64
     x = turn[p] * x + turn[p + FACES] * jnp.where(real, -other, other)
     hi, lo = split2(x)
     lhs = jnp.concatenate([hi, lo, hi], axis=1)
-    y = jnp.dot(lhs, table[...], preferred_element_type=f32)
+    t_hi, t_lo = split2(table[...])
+    rhs = jnp.concatenate([t_hi, t_hi, t_lo], axis=0)
+    y = jnp.dot(lhs, rhs, preferred_element_type=f32)
     y = jnp.concatenate([y[:, :128], y[:, 128:]], axis=0)
     for c in range(3):
         out[c] = y[32 * c : 32 * c + STA_DEV]
@@ -219,13 +227,17 @@
 SMEM = pl.BlockSpec(memory_space=pltpu.SMEM)
 
 
-def call(kernel, shape, specs, *args, dtype=f32):
+HBM = pl.BlockSpec(memory_space=pltpu.HBM)
+
+
+def call(kernel, shape, specs, *args, dtype=f32, scratch=(), grant=32):
     return pl.pallas_call(
         kernel,
         out_shape=jax.ShapeDtypeStruct(shape, dtype),
         in_specs=specs,
         out_specs=VMEM,
-        compiler_params=pltpu.CompilerParams(vmem_limit_bytes=32 * 1024 * 1024),
+        scratch_shapes=scratch,
+        compiler_params=pltpu.CompilerParams(vmem_limit_bytes=grant * 1024 * 1024),
     )(*args)
 
 
@@ -233,12 +245,19 @@
     held = call(
         window_kernel,
         (HOLD, 128),
-        [SMEM, SMEM, VMEM, VMEM, VMEM],
+        [HBM] * 4,
         face_counts,
-        jnp.asarray(turns(WINDOWS)),
         slip_rate,
         patch_ids.reshape(1, CAP),
         jnp.asarray(analysis_table()),
+        scratch=[
+            pltpu.SMEM((1,), jnp.int32),
+            pltpu.VMEM((CAP, T // WINDOWS), bf16),
+            pltpu.VMEM((1, CAP), jnp.int32),
+            pltpu.VMEM((T // WINDOWS, 128), f32),
+            pltpu.SemaphoreType.DMA((4,)),
+        ],
+        grant=60,
     )
     held = lax.all_gather(held, "patch", axis_index_groups=CORE_PAIRS)
     blocks = call(route_kernel, (16, 24, 128), [VMEM], held)
@@ -247,13 +266,18 @@
     )
     copies = call(spread_kernel, (16, 24, 128), [VMEM], blocks)
     copies = lax.all_to_all(copies, "freq", 0, 0, tiled=True)
-    tiles = green.transpose(0, 2, 3, 1, 4).reshape(6, 3, STA_DEV, 2, 12, 128)
-    tiles = tiles.transpose(0, 1, 2, 4, 3, 5).reshape(6 * 3 * STA_DEV * 24, 128)
-    partial = call(
-        green_kernel, (48, 128), [VMEM, VMEM, VMEM], tiles, moments.T, copies
-    )
+    green = green.transpose(0, 2, 3, 1, 4).reshape(6 * 3 * STA_DEV, 2, OWN * BINS)
+    tiles = call(
+        moment_kernel,
+        (3 * STA_DEV, 24, 128),
+        [VMEM, VMEM],
+        green,
+        moments.T,
+        scratch=[pltpu.VMEM((6, 2, OWN * BINS), f32)],
+    )
+    partial = call(patch_kernel, (48, 128), [VMEM, VMEM], tiles, copies)
     pair = lax.all_gather(partial, "patch", axis_index_groups=CORE_PAIRS)
-    copies = call(spread_kernel, (16, 48, 128), [VMEM], pair)
+    copies = call(spread_half_kernel, (16, 48, 128), [VMEM], pair, dtype=bf16)
     copies = lax.all_to_all(
         copies, "patch", 0, 0, axis_index_groups=SAME_CORE, tiled=True
     )

time: 77 us -> 66.3 us (0.86)
  the two profiles are of different devices: /device:TPU:8 before, /device:TPU:64 now
where the time goes in v2:
time: 66.3 us; the launch traced here: 66 us
  blocking collectives  42.8 us (65%)
  waiting for transfers between devices  7.28 us (11%)
  starting transfers between devices  7.24 us (11%)
  Pallas kernels  5.94 us (9%)
  local copies, waits for them, and re-layouts  1.98 us (3%)
  between operations  0.73 us (1%)
    all_to_all x1, blocking collectives, local(): lax.all_to_all(blocks, 'patch', 0, 0, axis_index_groups=SAME_CORE, tiled=...  23 us
    all_to_all x1, blocking collectives, local(): lax.all_to_all(copies, 'patch', 0, 0, axis_index_groups=SAME_CORE, tiled=...  15.9 us
    all_to_all x1, waiting for transfers between devices, local(): copies = lax.all_to_all(copies, 'freq', 0, 0, tiled=True)  7.28 us
    all_to_all x1, starting transfers between devices, local(): copies = lax.all_to_all(copies, 'freq', 0, 0, tiled=True)  7.24 us
    pallas_call x7, Pallas kernels, call(): pl.pallas_call(kernel, out_shape=jax.ShapeDtypeStruct(shape, dtype), in_s...  5.94 us
    all_gather x1, blocking collectives, local(): held = lax.all_gather(held, 'patch', axis_index_groups=CORE_PAIRS)  2.09 us
    unnamed x8, local copies, waits for them, and re-layouts  1.98 us
    all_gather x1, blocking collectives, local(): pair = lax.all_gather(partial, 'patch', axis_index_groups=CORE_PAIRS)  1.85 us
  transfers between devices with their start and end apart: 1, of which 1 were waited for; matrix products, arithmetic and copies ran while one was open for 0% of the time, Pallas kernels for 2%

profile of v2, /device:TPU:64, one launch (start us, length us, event | category | flops | bytes accessed | tf_op | source)
XLA Modules:
  0.0 66.0 jit_solution(842694146552533460)
XLA Ops:
  0.0 0.0 copy-start.2
  0.7 1.8 %shard_map.83 = f32[96,128]{1,0:T(8,128)} custom-call(s32[1]{0:T(128)S(6)} %copy.9.count_hbm, bf16[84,256]{1,0:T(8,128)(2,1)} %slip_hbm.1, s32[1,84]{1,0:T(1,128)} %bitcast.11, f32[16,256,128]{2,1,0:T(8,128)} %constant.6.clone.table_hbm), custom_call_target="tpu_custom_call" | custom-call | tf_op jit(solution)/shard_map/pallas_call | solution.py:234
  2.4 2.1 %all-gather = f32[192,128]{1,0:T(8,128)S(1)} all-gather(f32[96,128]{1,0:T(8,128)} %shard_map.83), channel_id=2, replica_groups={{0,16},{32,48},{64,80},{96,112},{128,144},{160,176},{192,208},{224,240}..., dimensions={0}, use_global_device_ids=true | all-gather | bytes 147456 | tf_op jit(solution)/shard_map/all_gather | solution.py:262
  4.5 0.7 shard_map.84
  5.2 23.0 %all_to_all.15.got = f32[16,24,128]{2,1,0:T(8,128)S(1)} all-to-all(f32[16,24,128]{2,1,0:T(8,128)S(1)} %shard_map.84), channel_id=1, replica_groups={{0,32,64,96,128,160,192,224,256,288,320,352,384,416,448,480},{16,48,80,..., dimensions={0} | all-to-all | bytes 393216 | tf_op jit(solution)/shard_map/all_to_all | solution.py:264
  28.2 0.7 %shard_map.85 = f32[16,24,128]{2,1,0:T(8,128)} custom-call(f32[16,24,128]{2,1,0:T(8,128)S(1)} %all_to_all.15.got), custom_call_target="tpu_custom_call" | custom-call | tf_op jit(solution)/shard_map/pallas_call | solution.py:234
  28.9 7.2 %all-to-all-start.1 = ((f32[16,24,128]{2,1,0:T(8,128)}), f32[16,24,128]{2,1,0:T(8,128)S(1)}, u32[]{:S(2)}, u32[]{:S(2)}) async-start(f32[16,24,128]{2,1,0:T(8,128)} %shard_map.85), calls=%async_computation.1 | async-start | bytes 393216 | tf_op jit(solution)/shard_map/all_to_all | solution.py:268
  36.1 0.0 copy-done.2
  36.1 0.0 copy-start
  36.1 2.0 %copy-done = bf16[6,2,3,31,1536]{4,1,3,2,0:T(2,128)(2,1)S(1)} copy-done((bf16[6,2,3,31,1536]{4,1,3,2,0:T(2,128)(2,1)S(1)}, bf16[6,2,3,31,1536]{4,1,3,2,0:T(2,128)(2,1)}, u32[]{:S(2)}) %copy-start) | copy-done | bytes 3428376
  38.1 0.0 copy-start.3
  38.1 1.0 %shard_map.82.tiles = f32[93,24,128]{2,1,0:T(8,128)S(1)} custom-call(bf16[558,2,1536]{2,1,0:T(2,128)(2,1)S(1)} %bitcast.7, f32[6,48]{1,0:T(8,128)S(1)} %bitcast.10), custom_call_target="tpu_custom_call" | custom-call | tf_op jit(solution)/shard_map/pallas_call | solution.py:234
  39.1 0.0 copy-start.1
  39.2 7.3 %all-to-all-done.1.got = f32[16,24,128]{2,1,0:T(8,128)S(1)} async-done(((f32[16,24,128]{2,1,0:T(8,128)}), f32[16,24,128]{2,1,0:T(8,128)S(1)}, u32[]{:S(2)}, u32[]{:S(2)}) %all-to-all-start.1) | async-done | bytes 196640 | tf_op jit(solution)/shard_map/all_to_all | solution.py:268
  46.4 0.4 shard_map.86
  46.8 1.8 %all-gather.1 = f32[96,128]{1,0:T(8,128)S(1)} all-gather(f32[48,128]{1,0:T(8,128)S(1)} %shard_map.86), channel_id=3, replica_groups={{0,16},{32,48},{64,80},{96,112},{128,144},{160,176},{192,208},{224,240}..., dimensions={0}, use_global_device_ids=true | all-gather | bytes 73728 | tf_op jit(solution)/shard_map/all_gather | solution.py:279
  48.7 15.9 %all_to_all.16.got = bf16[16,48,128]{2,1,0:T(8,128)(2,1)S(1)} all-to-all(bf16[16,48,128]{2,1,0:T(8,128)(2,1)S(1)} %shard_map.87), channel_id=1, replica_groups={{0,32,64,96,128,160,192,224,256,288,320,352,384,416,448,480},{16,48,80,..., dimensions={0} | all-to-all | bytes 393216 | tf_op jit(solution)/shard_map/all_to_all | solution.py:281
  64.6 0.0 copy-done.3
  64.6 0.0 copy-done.1
  64.6 1.4 %shard_map.88 = f32[3,31,128]{2,1,0:T(8,128)} custom-call(f32[64]{0:T(128)S(1)} %copy-done.3, bf16[16,48,128]{2,1,0:T(8,128)(2,1)S(1)} %all_to_all.16.got, f32[128,256]{1,0:T(8,128)S(1)} %copy-done.1), custom_call_target="tpu_custom_call" | custom-call | tf_op jit(solution)/shard_map/pallas_call | solution.py:234
  (1 shorter events, 0.0 us)
Async XLA Ops:
  0.0 36.1 %copy-start.2 = (f32[48,6]{0,1:T(8,128)S(1)}, f32[48,6]{0,1:T(8,128)}, u32[]{:S(2)}) copy-start(f32[48,6]{0,1:T(8,128)} %param.11) | copy-start | bytes 3460
  28.9 17.6 %all-to-all-start.1 = ((f32[16,24,128]{2,1,0:T(8,128)}), f32[16,24,128]{2,1,0:T(8,128)S(1)}, u32[]{:S(2)}, u32[]{:S(2)}) async-start(f32[16,24,128]{2,1,0:T(8,128)} %shard_map.85), calls=%async_computation.1 | async-start | bytes 393216 | tf_op jit(solution)/shard_map/all_to_all | solution.py:268
  36.1 2.0 %copy-start = (bf16[6,2,3,31,1536]{4,1,3,2,0:T(2,128)(2,1)S(1)}, bf16[6,2,3,31,1536]{4,1,3,2,0:T(2,128)(2,1)}, u32[]{:S(2)}) copy-start(bf16[6,2,3,31,1536]{4,1,3,2,0:T(2,128)(2,1)} %param.12) | copy-start | bytes 10285060
  38.1 26.5 %copy-start.3 = (f32[64]{0:T(128)S(1)}, f32[64]{0:T(128)}, u32[]{:S(2)}) copy-start(f32[64]{0:T(128)} %constant.7.clone.turn) | copy-start | bytes 772
  39.1 25.4 %copy-start.1 = (f32[128,256]{1,0:T(8,128)S(1)}, f32[128,256]{1,0:T(8,128)}, u32[]{:S(2)}) copy-start(f32[128,256]{1,0:T(8,128)} %constant.8.clone.table) | copy-start | bytes 393220

commit v3 on v2

--- a/solution.py
+++ b/solution.py
@@ -21,9 +21,13 @@
 
 CORE_PAIRS = [[2 * d, 2 * d + 1] for d in range(16)]
 SAME_CORE = [[2 * d + c for d in range(16)] for c in range(2)]
+SAME_CORE_Z = [[16 * x + 2 * z + c for z in range(8) for x in range(2)] for c in range(2)]
+
+CODE_SCALE = 2.0**56
 
 f32 = jnp.float32
 bf16 = jnp.bfloat16
+f16 = jnp.float16
 
 
 def split2(x):
@@ -56,7 +60,8 @@
 
 def turns(n):
     a = 2.0 * np.pi * np.arange(n) / n
-    return np.concatenate([np.cos(a), np.sin(a)]).astype(np.float32)
+    both = np.stack([np.cos(a), np.sin(a)], axis=1).astype(np.float32)
+    return np.broadcast_to(both[:, :, None], (n, 2, 128)).copy()
 
 
 def lanes(shape):
@@ -65,27 +70,36 @@
 
 def rows(shape):
     return lax.broadcasted_iota(jnp.int32, shape, len(shape) - 2)
+
+
+def encode(x):
+    root = jnp.sqrt(jnp.sqrt(jnp.abs(x) * CODE_SCALE))
+    return jnp.where(x < 0.0, -root, root)
+
+
+def decode(code):
+    square = code * code
+    return jnp.where(code < 0.0, -square, square) * square * (1.0 / CODE_SCALE)
 
 
 def window_kernel(count_hbm, slip_hbm, ids_hbm, table_hbm, out, count, slip, ids, table, sems):
     q = lax.axis_index("freq")
     copies = [
-        pltpu.make_async_copy(count_hbm, count, sems.at[0]),
-        pltpu.make_async_copy(ids_hbm, ids, sems.at[1]),
-        pltpu.make_async_copy(slip_hbm, slip, sems.at[2]),
-        pltpu.make_async_copy(table_hbm.at[q], table, sems.at[3]),
+        pltpu.make_async_copy(table_hbm.at[q], table, sems.at[0]),
+        pltpu.make_async_copy(slip_hbm, slip, sems.at[1]),
+        pltpu.make_async_copy(ids_hbm, ids, sems.at[2]),
+        pltpu.make_async_copy(count_hbm, count, sems.at[3]),
     ]
     for copy in copies:
         copy.start()
+    out[CAP:ID_ROW, :] = jnp.zeros((ID_ROW - CAP, 128), f32)
+    out[ID_ROW:HOLD, :] = jnp.full((HOLD - ID_ROW, 128), -1.0, f32)
     for copy in copies:
         copy.wait()
     both = jnp.concatenate(split2(table[...]), axis=1)
     r = jnp.dot(slip[...], both, preferred_element_type=f32)
-    x = r[:, :128] + r[:, 128:]
-    out[0:CAP, :] = jnp.where(rows((CAP, 128)) < count[0], x, 0.0)
-    out[ID_ROW:HOLD, :] = jnp.full((HOLD - ID_ROW, 128), -1.0, f32)
-    out[CAP:ID_ROW, :] = jnp.zeros((ID_ROW - CAP, 128), f32)
-    live = lanes((1, CAP)) < count[0]
+    out[0:CAP, :] = encode(r[:, :128] + r[:, 128:])
+    live = lanes((1, CAP)) < count[...]
     out[ID_ROW : ID_ROW + 1, 0:CAP] = jnp.where(live, ids[...].astype(f32), -1.0)
 
 
@@ -95,9 +109,11 @@
     r = rows((n, 128))
     d = lax.shift_right_logical(r * 2731, 16)
     j = lax.shift_right_logical(r - 24 * d, 1)
-    base = (96 * d + 4 * j).astype(f32)
+    base = (768 * (d & 1) + 96 * lax.shift_right_logical(d, 1) + 4 * j).astype(f32)
+    base = base + 48.0 * core
     block = lax.shift_right_logical(lanes((HOLD, 256)), 5) % 4
     odd = lax.rem(lax.shift_right_logical(lanes((HOLD, 128)), 5), 2) == 1
+    pad = jnp.zeros((128 - HOLD, 256), f32)
     left, right_hi, right_lo = [], [], []
     for k in range(2):
         x = held[k]
@@ -105,15 +121,11 @@
         im = jnp.where(odd, x, pltpu.roll(x, 96, 1))
         hi, lo = split2(jnp.concatenate([re, im], axis=1))
         hi, lo = hi.astype(f32), lo.astype(f32)
-        owner = held[k, ID_ROW : ID_ROW + 1, :]
-        ahead = owner - base - 48.0 * core
-        pad = jnp.zeros((128 - HOLD, 256), f32)
+        ahead = held[k, ID_ROW : ID_ROW + 1, :] - base
         for b in range(4):
             left.append(jnp.where(ahead == float(b), 1.0, 0.0))
-            right_hi.append(jnp.where(block == b, hi, 0.0))
-            right_hi.append(pad)
-            right_lo.append(jnp.where(block == b, lo, 0.0))
-            right_lo.append(pad)
+            right_hi += [jnp.where(block == b, hi, 0.0), pad]
+            right_lo += [jnp.where(block == b, lo, 0.0), pad]
     lhs = jnp.concatenate(left, axis=1).astype(bf16)
     rhs_hi = jnp.concatenate(right_hi, axis=0).astype(bf16)
     rhs_lo = jnp.concatenate(right_lo, axis=0).astype(bf16)
@@ -122,11 +134,6 @@
     )
     even = lax.rem(r, 2) == 0
     out[...] = jnp.where(even, got[:, :128], got[:, 128:]).reshape(16, 24, 128)
-
-
-def spread_kernel(got, out):
-    total = jnp.sum(got[...], axis=0)
-    out[...] = jnp.broadcast_to(total[None], out.shape)
 
 
 def sublane_sums(parts):
@@ -172,7 +179,7 @@
 
 
 def patch_kernel(tiles, got, out):
-    s = jnp.sum(got[...], axis=0)
+    s = got[...]
     even = lax.rem(rows((24, 128)), 2) == 0
     for_re = jnp.where(even, s, -s)
     for_im = jnp.where(even, pltpu.roll(s, 23, 0), pltpu.roll(s, 1, 0))
@@ -212,7 +219,8 @@
     x = jnp.sum(got[...].astype(f32), axis=0)
     other = pltpu.roll(x, 64, 1)
     real = lanes((48, 128)) < 64
-    x = turn[p] * x + turn[p + FACES] * jnp.where(real, -other, other)
+    turned = turn[p]
+    x = turned[0:1] * x + turned[1:2] * jnp.where(real, -other, other)
     hi, lo = split2(x)
     lhs = jnp.concatenate([hi, lo, hi], axis=1)
     t_hi, t_lo = split2(table[...])
@@ -246,12 +254,12 @@
         window_kernel,
         (HOLD, 128),
         [HBM] * 4,
-        face_counts,
+        face_counts.reshape(1, 1),
         slip_rate,
         patch_ids.reshape(1, CAP),
         jnp.asarray(analysis_table()),
         scratch=[
-            pltpu.SMEM((1,), jnp.int32),
+            pltpu.VMEM((1, 1), jnp.int32),
             pltpu.VMEM((CAP, T // WINDOWS), bf16),
             pltpu.VMEM((1, CAP), jnp.int32),
             pltpu.VMEM((T // WINDOWS, 128), f32),
@@ -260,12 +268,14 @@
         grant=60,
     )
     held = lax.all_gather(held, "patch", axis_index_groups=CORE_PAIRS)
-    blocks = call(route_kernel, (16, 24, 128), [VMEM], held)
+    blocks = call(route_kernel, (16, 24, 128), [VMEM], held).astype(f16)
     blocks = lax.all_to_all(
-        blocks, "patch", 0, 0, axis_index_groups=SAME_CORE, tiled=True
-    )
-    copies = call(spread_kernel, (16, 24, 128), [VMEM], blocks)
-    copies = lax.all_to_all(copies, "freq", 0, 0, tiled=True)
+        blocks, "patch", 0, 0, axis_index_groups=SAME_CORE_Z, tiled=True
+    )
+    code = jnp.sum(blocks.astype(f32), axis=0).astype(f16)
+    codes = jnp.broadcast_to(code[None], (WINDOWS, 24, 128))
+    codes = lax.all_to_all(codes, "freq", 0, 0, tiled=True)
+    spectra = jnp.sum(decode(codes.astype(f32)), axis=0)
     green = green.transpose(0, 2, 3, 1, 4).reshape(6 * 3 * STA_DEV, 2, OWN * BINS)
     tiles = call(
         moment_kernel,
@@ -275,7 +285,7 @@
         moments.T,
         scratch=[pltpu.VMEM((6, 2, OWN * BINS), f32)],
     )
-    partial = call(patch_kernel, (48, 128), [VMEM, VMEM], tiles, copies)
+    partial = call(patch_kernel, (48, 128), [VMEM, VMEM], tiles, spectra)
     pair = lax.all_gather(partial, "patch", axis_index_groups=CORE_PAIRS)
     copies = call(spread_half_kernel, (16, 48, 128), [VMEM], pair, dtype=bf16)
     copies = lax.all_to_all(
@@ -284,7 +294,7 @@
     return call(
         series_kernel,
         (3, STA_DEV, 128),
-        [SMEM, VMEM, VMEM],
+        [VMEM, VMEM, VMEM],
         jnp.asarray(turns(FACES)),
         copies,
         jnp.asarray(synthesis_table()),

time: 66.3 us -> 62.7 us (0.946)
  blocking collectives: 42.8 us -> 40.7 us
  Pallas kernels: 5.94 us -> 4.71 us
  waiting for transfers between devices: 7.28 us -> 6.29 us
    all_to_all x1, blocking collectives: 23 us -> 21.6 us  [local(): lax.all_to_all(blocks, 'patch', 0, 0, axis_index_groups=SAME_CORE_Z, tile...]
    pallas_call x7 -> x6, Pallas kernels: 5.94 us -> 4.71 us  [call(): pl.pallas_call(kernel, out_shape=jax.ShapeDtypeStruct(shape, dtype), in_s...]
    all_to_all x1, waiting for transfers between devices: 7.28 us -> 6.29 us  [local(): codes = lax.all_to_all(codes, 'freq', 0, 0, tiled=True)]
    all_to_all x1, blocking collectives: 15.9 us -> 15.1 us  [local(): lax.all_to_all(copies, 'patch', 0, 0, axis_index_groups=SAME_CORE, tiled=...]
where the time goes in v3:
time: 62.7 us; the launch traced here: 62.4 us
  blocking collectives  40.7 us (65%)
  starting transfers between devices  7.24 us (12%)
  waiting for transfers between devices  6.29 us (10%)
  Pallas kernels  4.71 us (8%)
  local copies, waits for them, and re-layouts  2.63 us (4%)
  between operations  0.74 us (1%)
    all_to_all x1, blocking collectives, local(): lax.all_to_all(blocks, 'patch', 0, 0, axis_index_groups=SAME_CORE_Z, tile...  21.6 us
    all_to_all x1, blocking collectives, local(): lax.all_to_all(copies, 'patch', 0, 0, axis_index_groups=SAME_CORE, tiled=...  15.1 us
    all_to_all x1, starting transfers between devices, local(): codes = lax.all_to_all(codes, 'freq', 0, 0, tiled=True)  7.24 us
    all_to_all x1, waiting for transfers between devices, local(): codes = lax.all_to_all(codes, 'freq', 0, 0, tiled=True)  6.29 us
    pallas_call x6, Pallas kernels, call(): pl.pallas_call(kernel, out_shape=jax.ShapeDtypeStruct(shape, dtype), in_s...  4.71 us
    all_gather x1, blocking collectives, local(): held = lax.all_gather(held, 'patch', axis_index_groups=CORE_PAIRS)  2.09 us
    unnamed x8, local copies, waits for them, and re-layouts  1.98 us
    all_gather x1, blocking collectives, local(): pair = lax.all_gather(partial, 'patch', axis_index_groups=CORE_PAIRS)  1.85 us
  transfers between devices with their start and end apart: 1, of which 1 were waited for; matrix products, arithmetic and copies ran while one was open for 0% of the time, Pallas kernels for 2%

profile of v3, /device:TPU:64, one launch (start us, length us, event | category | flops | bytes accessed | tf_op | source)
XLA Modules:
  0.0 62.4 jit_solution(114650734980211797)
XLA Ops:
  0.0 0.0 copy-start.3
  0.7 1.8 %shard_map.83 = f32[96,128]{1,0:T(8,128)} custom-call(s32[1,1]{1,0:T(1,128)} %bitcast.8.count_hbm, bf16[84,256]{1,0:T(8,128)(2,1)} %slip_hbm.1, s32[1,84]{1,0:T(1,128)} %bitcast.13, f32[16,256,128]{2,1,0:T(8,128)} %constant.4.clone.table_hbm), custom_call_target="tpu_custom_call" | custom-call | tf_op jit(solution)/shard_map/pallas_call | solution.py:242
  2.4 2.1 %all-gather = f32[192,128]{1,0:T(8,128)S(1)} all-gather(f32[96,128]{1,0:T(8,128)} %shard_map.83), channel_id=2, replica_groups={{0,16},{32,48},{64,80},{96,112},{128,144},{160,176},{192,208},{224,240}..., dimensions={0}, use_global_device_ids=true | all-gather | bytes 147456 | tf_op jit(solution)/shard_map/all_gather | solution.py:270
  4.5 0.7 %shard_map.84 = f32[16,24,128]{2,1,0:T(8,128)S(1)} custom-call(f32[2,96,128]{2,1,0:T(8,128)S(1)} %bitcast.10), custom_call_target="tpu_custom_call" | custom-call | tf_op jit(solution)/shard_map/pallas_call | solution.py:242
  5.2 21.6 %all_to_all.15 = f16[16,24,128]{2,1,0:T(8,128)(2,1)S(1)} all-to-all(f16[16,24,128]{2,1,0:T(8,128)(2,1)S(1)} %convert_element_type.16), channel_id=1, replica_groups={{0,256,32,288,64,320,96,352,128,384,160,416,192,448,224,480},{16,272,48..., dimensions={0} | all-to-all | bytes 196608 | tf_op jit(solution)/shard_map/all_to_all | solution.py:272
  26.9 0.7 %broadcast_in_dim.2 = f16[16,24,128]{2,1,0:T(8,128)(2,1)} broadcast(f16[24,128]{1,0:T(8,128)(2,1)S(1)} %convert_element_type.18), dimensions={1,2} | broadcast | bytes 104448 | tf_op jit(solution)/shard_map/broadcast_in_dim | solution.py:276
  27.6 7.2 %all-to-all-start.1 = ((f16[16,24,128]{2,1,0:T(8,128)(2,1)}), f16[16,24,128]{2,1,0:T(8,128)(2,1)S(1)}, u32[]{:S(2)}, u32[]{:S(2)}) async-start(f16[16,24,128]{2,1,0:T(8,128)(2,1)} %broadcast_in_dim.2), calls=%async_computation.1 | async-start | bytes 196608 | tf_op jit(solution)/shard_map/all_to_all | solution.py:277
  34.8 0.0 copy-done.3
  34.8 0.0 copy-start
  34.8 2.0 %copy-done = bf16[6,2,3,31,1536]{4,1,3,2,0:T(2,128)(2,1)S(1)} copy-done((bf16[6,2,3,31,1536]{4,1,3,2,0:T(2,128)(2,1)S(1)}, bf16[6,2,3,31,1536]{4,1,3,2,0:T(2,128)(2,1)}, u32[]{:S(2)}) %copy-start) | copy-done | bytes 3428376
  36.8 0.0 copy-start.1
  36.8 0.0 copy-start.2
  36.8 1.0 %shard_map.82.tiles = f32[93,24,128]{2,1,0:T(8,128)S(1)} custom-call(bf16[558,2,1536]{2,1,0:T(2,128)(2,1)S(1)} %bitcast.9, f32[6,48]{1,0:T(8,128)S(1)} %bitcast.12), custom_call_target="tpu_custom_call" | custom-call | tf_op jit(solution)/shard_map/pallas_call | solution.py:242
  37.8 6.3 %all-to-all-done.1 = f16[16,24,128]{2,1,0:T(8,128)(2,1)S(1)} async-done(((f16[16,24,128]{2,1,0:T(8,128)(2,1)}), f16[16,24,128]{2,1,0:T(8,128)(2,1)S(1)}, u32[]{:S(2)}, u32[]{:S(2)}) %all-to-all-start.1) | async-done | bytes 98336 | tf_op jit(solution)/shard_map/all_to_all | solution.py:277
  44.1 0.1 fusion.1.got
  44.2 0.4 shard_map.85
  44.6 1.8 %all-gather.1 = f32[96,128]{1,0:T(8,128)S(1)} all-gather(f32[48,128]{1,0:T(8,128)S(1)} %shard_map.85), channel_id=3, replica_groups={{0,16},{32,48},{64,80},{96,112},{128,144},{160,176},{192,208},{224,240}..., dimensions={0}, use_global_device_ids=true | all-gather | bytes 73728 | tf_op jit(solution)/shard_map/all_gather | solution.py:289
  46.4 15.1 %all_to_all.16.got = bf16[16,48,128]{2,1,0:T(8,128)(2,1)S(1)} all-to-all(bf16[16,48,128]{2,1,0:T(8,128)(2,1)S(1)} %shard_map.86), channel_id=1, replica_groups={{0,32,64,96,128,160,192,224,256,288,320,352,384,416,448,480},{16,48,80,..., dimensions={0} | all-to-all | bytes 393216 | tf_op jit(solution)/shard_map/all_to_all | solution.py:291
  61.5 0.0 copy-done.1
  61.5 0.0 copy-done.2
  61.5 0.9 %shard_map.87 = f32[3,31,128]{2,1,0:T(8,128)} custom-call(f32[32,2,128]{2,1,0:T(2,128)S(1)} %copy-done.2, bf16[16,48,128]{2,1,0:T(8,128)(2,1)S(1)} %all_to_all.16.got, f32[128,256]{1,0:T(8,128)S(1)} %copy-done.1), custom_call_target="tpu_custom_call" | custom-call | tf_op jit(solution)/shard_map/pallas_call | solution.py:242
  (4 shorter events, 0.1 us)
Async XLA Ops:
  0.0 34.8 %copy-start.3 = (f32[48,6]{0,1:T(8,128)S(1)}, f32[48,6]{0,1:T(8,128)}, u32[]{:S(2)}) copy-start(f32[48,6]{0,1:T(8,128)} %param.11) | copy-start | bytes 3460
  27.6 16.6 %all-to-all-start.1 = ((f16[16,24,128]{2,1,0:T(8,128)(2,1)}), f16[16,24,128]{2,1,0:T(8,128)(2,1)S(1)}, u32[]{:S(2)}, u32[]{:S(2)}) async-start(f16[16,24,128]{2,1,0:T(8,128)(2,1)} %broadcast_in_dim.2), calls=%async_computation.1 | async-start | bytes 196608 | tf_op jit(solution)/shard_map/all_to_all | solution.py:277
  34.8 2.0 %copy-start = (bf16[6,2,3,31,1536]{4,1,3,2,0:T(2,128)(2,1)S(1)}, bf16[6,2,3,31,1536]{4,1,3,2,0:T(2,128)(2,1)}, u32[]{:S(2)}) copy-start(bf16[6,2,3,31,1536]{4,1,3,2,0:T(2,128)(2,1)} %param.12) | copy-start | bytes 10285060
  36.8 24.7 %copy-start.1 = (f32[128,256]{1,0:T(8,128)S(1)}, f32[128,256]{1,0:T(8,128)}, u32[]{:S(2)}) copy-start(f32[128,256]{1,0:T(8,128)} %constant.13.clone.table) | copy-start | bytes 393220
  36.8 24.7 %copy-start.2 = (f32[32,2,128]{2,1,0:T(2,128)S(1)}, f32[32,2,128]{2,1,0:T(2,128)}, u32[]{:S(2)}) copy-start(f32[32,2,128]{2,1,0:T(2,128)} %constant.12.clone.turn) | copy-start | bytes 98308

commit v4 on v3

--- a/solution.py
+++ b/solution.py
@@ -22,6 +22,8 @@
 CORE_PAIRS = [[2 * d, 2 * d + 1] for d in range(16)]
 SAME_CORE = [[2 * d + c for d in range(16)] for c in range(2)]
 SAME_CORE_Z = [[16 * x + 2 * z + c for z in range(8) for x in range(2)] for c in range(2)]
+DOWN_Y = [4, 3, 2, 1, 0, 7, 6, 5]
+WINDOW_GROUP = [[2 * y + x for x in range(2) for y in DOWN_Y]]
 
 CODE_SCALE = 2.0**56
 
@@ -274,7 +276,9 @@
     )
     code = jnp.sum(blocks.astype(f32), axis=0).astype(f16)
     codes = jnp.broadcast_to(code[None], (WINDOWS, 24, 128))
-    codes = lax.all_to_all(codes, "freq", 0, 0, tiled=True)
+    codes = lax.all_to_all(
+        codes, "freq", 0, 0, axis_index_groups=WINDOW_GROUP, tiled=True
+    )
     spectra = jnp.sum(decode(codes.astype(f32)), axis=0)
     green = green.transpose(0, 2, 3, 1, 4).reshape(6 * 3 * STA_DEV, 2, OWN * BINS)
     tiles = call(

time: 62.7 us -> 59.4 us (0.947)
  the two profiles are of different devices: /device:TPU:64 before, /device:TPU:8 now
where the time goes in v4:
time: 59.4 us; the launch traced here: 59.1 us
  blocking collectives  40.8 us (69%)
  starting transfers between devices  8.13 us (14%)
  Pallas kernels  4.71 us (8%)
  local copies, waits for them, and re-layouts  2.63 us (4%)
  waiting for transfers between devices  1.94 us (3%)
  between operations  0.73 us (1%)
    all_to_all x1, blocking collectives, local(): lax.all_to_all(blocks, 'patch', 0, 0, axis_index_groups=SAME_CORE_Z, tile...  23.5 us
    all_to_all x1, blocking collectives, local(): lax.all_to_all(copies, 'patch', 0, 0, axis_index_groups=SAME_CORE, tiled=...  13.4 us
    all_to_all x1, starting transfers between devices, local(): lax.all_to_all(codes, 'freq', 0, 0, axis_index_groups=WINDOW_GROUP, tiled...  8.13 us
    pallas_call x6, Pallas kernels, call(): pl.pallas_call(kernel, out_shape=jax.ShapeDtypeStruct(shape, dtype), in_s...  4.71 us
    all_gather x1, blocking collectives, local(): held = lax.all_gather(held, 'patch', axis_index_groups=CORE_PAIRS)  2.09 us
    unnamed x8, local copies, waits for them, and re-layouts  1.98 us
    all_to_all x1, waiting for transfers between devices, local(): lax.all_to_all(codes, 'freq', 0, 0, axis_index_groups=WINDOW_GROUP, tiled...  1.94 us
    all_gather x1, blocking collectives, local(): pair = lax.all_gather(partial, 'patch', axis_index_groups=CORE_PAIRS)  1.85 us
  transfers between devices with their start and end apart: 1, of which 1 were waited for; matrix products, arithmetic and copies ran while one was open for 0% of the time, Pallas kernels for 2%

profile of v4, /device:TPU:8, one launch (start us, length us, event | category | flops | bytes accessed | tf_op | source)
XLA Modules:
  0.0 59.1 jit_solution(12161534921663154421)
XLA Ops:
  0.0 0.0 copy-start.3
  0.7 1.8 %shard_map.83 = f32[96,128]{1,0:T(8,128)} custom-call(s32[1,1]{1,0:T(1,128)} %bitcast.8.count_hbm, bf16[84,256]{1,0:T(8,128)(2,1)} %slip_hbm.1, s32[1,84]{1,0:T(1,128)} %bitcast.13, f32[16,256,128]{2,1,0:T(8,128)} %constant.4.clone.table_hbm), custom_call_target="tpu_custom_call" | custom-call | tf_op jit(solution)/shard_map/pallas_call | solution.py:244
  2.4 2.1 %all-gather = f32[192,128]{1,0:T(8,128)S(1)} all-gather(f32[96,128]{1,0:T(8,128)} %shard_map.83), channel_id=2, replica_groups={{0,16},{32,48},{64,80},{96,112},{128,144},{160,176},{192,208},{224,240}..., dimensions={0}, use_global_device_ids=true | all-gather | bytes 147456 | tf_op jit(solution)/shard_map/all_gather | solution.py:272
  4.5 0.7 %shard_map.84 = f32[16,24,128]{2,1,0:T(8,128)S(1)} custom-call(f32[2,96,128]{2,1,0:T(8,128)S(1)} %bitcast.10), custom_call_target="tpu_custom_call" | custom-call | tf_op jit(solution)/shard_map/pallas_call | solution.py:244
  5.2 23.5 %all_to_all.15 = f16[16,24,128]{2,1,0:T(8,128)(2,1)S(1)} all-to-all(f16[16,24,128]{2,1,0:T(8,128)(2,1)S(1)} %convert_element_type.16), channel_id=1, replica_groups={{0,256,32,288,64,320,96,352,128,384,160,416,192,448,224,480},{16,272,48..., dimensions={0} | all-to-all | bytes 196608 | tf_op jit(solution)/shard_map/all_to_all | solution.py:274
  28.8 0.7 %broadcast_in_dim.2 = f16[16,24,128]{2,1,0:T(8,128)(2,1)} broadcast(f16[24,128]{1,0:T(8,128)(2,1)S(1)} %convert_element_type.18), dimensions={1,2} | broadcast | bytes 104448 | tf_op jit(solution)/shard_map/broadcast_in_dim | solution.py:278
  29.4 8.1 %all-to-all-start.1 = ((f16[16,24,128]{2,1,0:T(8,128)(2,1)}), f16[16,24,128]{2,1,0:T(8,128)(2,1)S(1)}, u32[]{:S(2)}, u32[]{:S(2)}) async-start(f16[16,24,128]{2,1,0:T(8,128)(2,1)} %broadcast_in_dim.2), calls=%async_computation.1 | async-start | bytes 196608 | tf_op jit(solution)/shard_map/all_to_all | solution.py:279
  37.6 0.0 copy-done.3
  37.6 0.0 copy-start
  37.6 2.0 %copy-done = bf16[6,2,3,31,1536]{4,1,3,2,0:T(2,128)(2,1)S(1)} copy-done((bf16[6,2,3,31,1536]{4,1,3,2,0:T(2,128)(2,1)S(1)}, bf16[6,2,3,31,1536]{4,1,3,2,0:T(2,128)(2,1)}, u32[]{:S(2)}) %copy-start) | copy-done | bytes 3428376
  39.5 0.0 copy-start.1
  39.5 0.0 copy-start.2
  39.5 1.0 %shard_map.82.tiles = f32[93,24,128]{2,1,0:T(8,128)S(1)} custom-call(bf16[558,2,1536]{2,1,0:T(2,128)(2,1)S(1)} %bitcast.9, f32[6,48]{1,0:T(8,128)S(1)} %bitcast.12), custom_call_target="tpu_custom_call" | custom-call | tf_op jit(solution)/shard_map/pallas_call | solution.py:244
  40.6 1.9 %all-to-all-done.1 = f16[16,24,128]{2,1,0:T(8,128)(2,1)S(1)} async-done(((f16[16,24,128]{2,1,0:T(8,128)(2,1)}), f16[16,24,128]{2,1,0:T(8,128)(2,1)S(1)}, u32[]{:S(2)}, u32[]{:S(2)}) %all-to-all-start.1) | async-done | bytes 98336 | tf_op jit(solution)/shard_map/all_to_all | solution.py:279
  42.5 0.1 fusion.1.got
  42.6 0.4 shard_map.85
  43.0 1.8 %all-gather.1 = f32[96,128]{1,0:T(8,128)S(1)} all-gather(f32[48,128]{1,0:T(8,128)S(1)} %shard_map.85), channel_id=3, replica_groups={{0,16},{32,48},{64,80},{96,112},{128,144},{160,176},{192,208},{224,240}..., dimensions={0}, use_global_device_ids=true | all-gather | bytes 73728 | tf_op jit(solution)/shard_map/all_gather | solution.py:293
  44.8 13.4 %all_to_all.16.got = bf16[16,48,128]{2,1,0:T(8,128)(2,1)S(1)} all-to-all(bf16[16,48,128]{2,1,0:T(8,128)(2,1)S(1)} %shard_map.86), channel_id=1, replica_groups={{0,32,64,96,128,160,192,224,256,288,320,352,384,416,448,480},{16,48,80,..., dimensions={0} | all-to-all | bytes 393216 | tf_op jit(solution)/shard_map/all_to_all | solution.py:295
  58.2 0.0 copy-done.1
  58.2 0.0 copy-done.2
  58.2 0.9 %shard_map.87 = f32[3,31,128]{2,1,0:T(8,128)} custom-call(f32[32,2,128]{2,1,0:T(2,128)S(1)} %copy-done.2, bf16[16,48,128]{2,1,0:T(8,128)(2,1)S(1)} %all_to_all.16.got, f32[128,256]{1,0:T(8,128)S(1)} %copy-done.1), custom_call_target="tpu_custom_call" | custom-call | tf_op jit(solution)/shard_map/pallas_call | solution.py:244
  (4 shorter events, 0.1 us)
Async XLA Ops:
  0.0 37.6 %copy-start.3 = (f32[48,6]{0,1:T(8,128)S(1)}, f32[48,6]{0,1:T(8,128)}, u32[]{:S(2)}) copy-start(f32[48,6]{0,1:T(8,128)} %param.11) | copy-start | bytes 3460
  29.4 13.1 %all-to-all-start.1 = ((f16[16,24,128]{2,1,0:T(8,128)(2,1)}), f16[16,24,128]{2,1,0:T(8,128)(2,1)S(1)}, u32[]{:S(2)}, u32[]{:S(2)}) async-start(f16[16,24,128]{2,1,0:T(8,128)(2,1)} %broadcast_in_dim.2), calls=%async_computation.1 | async-start | bytes 196608 | tf_op jit(solution)/shard_map/all_to_all | solution.py:279
  37.6 2.0 %copy-start = (bf16[6,2,3,31,1536]{4,1,3,2,0:T(2,128)(2,1)S(1)}, bf16[6,2,3,31,1536]{4,1,3,2,0:T(2,128)(2,1)}, u32[]{:S(2)}) copy-start(bf16[6,2,3,31,1536]{4,1,3,2,0:T(2,128)(2,1)} %param.12) | copy-start | bytes 10285060
  39.5 18.7 %copy-start.1 = (f32[128,256]{1,0:T(8,128)S(1)}, f32[128,256]{1,0:T(8,128)}, u32[]{:S(2)}) copy-start(f32[128,256]{1,0:T(8,128)} %constant.13.clone.table) | copy-start | bytes 393220
  39.5 18.7 %copy-start.2 = (f32[32,2,128]{2,1,0:T(2,128)S(1)}, f32[32,2,128]{2,1,0:T(2,128)}, u32[]{:S(2)}) copy-start(f32[32,2,128]{2,1,0:T(2,128)} %constant.12.clone.turn) | copy-start | bytes 98308

commit v5 on v4

--- a/solution.py
+++ b/solution.py
@@ -21,9 +21,8 @@
 
 CORE_PAIRS = [[2 * d, 2 * d + 1] for d in range(16)]
 SAME_CORE = [[2 * d + c for d in range(16)] for c in range(2)]
-SAME_CORE_Z = [[16 * x + 2 * z + c for z in range(8) for x in range(2)] for c in range(2)]
 DOWN_Y = [4, 3, 2, 1, 0, 7, 6, 5]
-WINDOW_GROUP = [[2 * y + x for x in range(2) for y in DOWN_Y]]
+WINDOW_GROUP = [[2 * y + x for x in (1, 0) for y in DOWN_Y]]
 
 CODE_SCALE = 2.0**56
 
@@ -111,7 +110,7 @@
     r = rows((n, 128))
     d = lax.shift_right_logical(r * 2731, 16)
     j = lax.shift_right_logical(r - 24 * d, 1)
-    base = (768 * (d & 1) + 96 * lax.shift_right_logical(d, 1) + 4 * j).astype(f32)
+    base = (96 * d + 4 * j).astype(f32)
     base = base + 48.0 * core
     block = lax.shift_right_logical(lanes((HOLD, 256)), 5) % 4
     odd = lax.rem(lax.shift_right_logical(lanes((HOLD, 128)), 5), 2) == 1
@@ -272,7 +271,7 @@
     held = lax.all_gather(held, "patch", axis_index_groups=CORE_PAIRS)
     blocks = call(route_kernel, (16, 24, 128), [VMEM], held).astype(f16)
     blocks = lax.all_to_all(
-        blocks, "patch", 0, 0, axis_index_groups=SAME_CORE_Z, tiled=True
+        blocks, "patch", 0, 0, axis_index_groups=SAME_CORE, tiled=True
     )
     code = jnp.sum(blocks.astype(f32), axis=0).astype(f16)
     codes = jnp.broadcast_to(code[None], (WINDOWS, 24, 128))

time: 59.4 us -> 58.5 us (0.985)
  waiting for transfers between devices: 1.94 us -> 1.22 us
    all_to_all x1, blocking collectives: 23.5 us -> 22.7 us  [local(): lax.all_to_all(blocks, 'patch', 0, 0, axis_index_groups=SAME_CORE, tiled=...]
    all_to_all x1, waiting for transfers between devices: 1.94 us -> 1.22 us  [local(): lax.all_to_all(codes, 'freq', 0, 0, axis_index_groups=WINDOW_GROUP, tiled...]
where the time goes in v5:
time: 58.5 us; the launch traced here: 58.1 us
  blocking collectives  40.5 us (69%)
  starting transfers between devices  8.2 us (14%)
  Pallas kernels  4.71 us (8%)
  local copies, waits for them, and re-layouts  2.63 us (4%)
  waiting for transfers between devices  1.22 us (2%)
  between operations  0.73 us (1%)
    all_to_all x1, blocking collectives, local(): lax.all_to_all(blocks, 'patch', 0, 0, axis_index_groups=SAME_CORE, tiled=...  22.7 us
    all_to_all x1, blocking collectives, local(): lax.all_to_all(copies, 'patch', 0, 0, axis_index_groups=SAME_CORE, tiled=...  13.9 us
    all_to_all x1, starting transfers between devices, local(): lax.all_to_all(codes, 'freq', 0, 0, axis_index_groups=WINDOW_GROUP, tiled...  8.2 us
    pallas_call x6, Pallas kernels, call(): pl.pallas_call(kernel, out_shape=jax.ShapeDtypeStruct(shape, dtype), in_s...  4.71 us
    all_gather x1, blocking collectives, local(): held = lax.all_gather(held, 'patch', axis_index_groups=CORE_PAIRS)  2.09 us
    unnamed x8, local copies, waits for them, and re-layouts  1.98 us
    all_gather x1, blocking collectives, local(): pair = lax.all_gather(partial, 'patch', axis_index_groups=CORE_PAIRS)  1.85 us
    all_to_all x1, waiting for transfers between devices, local(): lax.all_to_all(codes, 'freq', 0, 0, axis_index_groups=WINDOW_GROUP, tiled...  1.22 us
  transfers between devices with their start and end apart: 1, of which 1 were waited for; matrix products, arithmetic and copies ran while one was open for 0% of the time, Pallas kernels for 2%

profile of v5, /device:TPU:8, one launch (start us, length us, event | category | flops | bytes accessed | tf_op | source)
XLA Modules:
  0.0 58.1 jit_solution(7598832004851014716)
XLA Ops:
  0.0 0.0 copy-start.3
  0.7 1.8 %shard_map.83 = f32[96,128]{1,0:T(8,128)} custom-call(s32[1,1]{1,0:T(1,128)} %bitcast.8.count_hbm, bf16[84,256]{1,0:T(8,128)(2,1)} %slip_hbm.1, s32[1,84]{1,0:T(1,128)} %bitcast.13, f32[16,256,128]{2,1,0:T(8,128)} %constant.4.clone.table_hbm), custom_call_target="tpu_custom_call" | custom-call | tf_op jit(solution)/shard_map/pallas_call | solution.py:243
  2.4 2.1 %all-gather = f32[192,128]{1,0:T(8,128)S(1)} all-gather(f32[96,128]{1,0:T(8,128)} %shard_map.83), channel_id=2, replica_groups={{0,16},{32,48},{64,80},{96,112},{128,144},{160,176},{192,208},{224,240}..., dimensions={0}, use_global_device_ids=true | all-gather | bytes 147456 | tf_op jit(solution)/shard_map/all_gather | solution.py:271
  4.5 0.7 %shard_map.84 = f32[16,24,128]{2,1,0:T(8,128)S(1)} custom-call(f32[2,96,128]{2,1,0:T(8,128)S(1)} %bitcast.10), custom_call_target="tpu_custom_call" | custom-call | tf_op jit(solution)/shard_map/pallas_call | solution.py:243
  5.2 22.7 %all_to_all.15 = f16[16,24,128]{2,1,0:T(8,128)(2,1)S(1)} all-to-all(f16[16,24,128]{2,1,0:T(8,128)(2,1)S(1)} %convert_element_type.16), channel_id=1, replica_groups={{0,32,64,96,128,160,192,224,256,288,320,352,384,416,448,480},{16,48,80,..., dimensions={0} | all-to-all | bytes 196608 | tf_op jit(solution)/shard_map/all_to_all | solution.py:273
  28.0 0.7 %broadcast_in_dim.2 = f16[16,24,128]{2,1,0:T(8,128)(2,1)} broadcast(f16[24,128]{1,0:T(8,128)(2,1)S(1)} %convert_element_type.18), dimensions={1,2} | broadcast | bytes 104448 | tf_op jit(solution)/shard_map/broadcast_in_dim | solution.py:277
  28.6 8.2 %all-to-all-start.1 = ((f16[16,24,128]{2,1,0:T(8,128)(2,1)}), f16[16,24,128]{2,1,0:T(8,128)(2,1)S(1)}, u32[]{:S(2)}, u32[]{:S(2)}) async-start(f16[16,24,128]{2,1,0:T(8,128)(2,1)} %broadcast_in_dim.2), calls=%async_computation.1 | async-start | bytes 196608 | tf_op jit(solution)/shard_map/all_to_all | solution.py:278
  36.8 0.0 copy-done.3
  36.9 0.0 copy-start
  36.9 2.0 %copy-done = bf16[6,2,3,31,1536]{4,1,3,2,0:T(2,128)(2,1)S(1)} copy-done((bf16[6,2,3,31,1536]{4,1,3,2,0:T(2,128)(2,1)S(1)}, bf16[6,2,3,31,1536]{4,1,3,2,0:T(2,128)(2,1)}, u32[]{:S(2)}) %copy-start) | copy-done | bytes 3428376
  38.8 0.0 copy-start.1
  38.8 0.0 copy-start.2
  38.8 1.0 %shard_map.82.tiles = f32[93,24,128]{2,1,0:T(8,128)S(1)} custom-call(bf16[558,2,1536]{2,1,0:T(2,128)(2,1)S(1)} %bitcast.9, f32[6,48]{1,0:T(8,128)S(1)} %bitcast.12), custom_call_target="tpu_custom_call" | custom-call | tf_op jit(solution)/shard_map/pallas_call | solution.py:243
  39.9 1.2 %all-to-all-done.1 = f16[16,24,128]{2,1,0:T(8,128)(2,1)S(1)} async-done(((f16[16,24,128]{2,1,0:T(8,128)(2,1)}), f16[16,24,128]{2,1,0:T(8,128)(2,1)S(1)}, u32[]{:S(2)}, u32[]{:S(2)}) %all-to-all-start.1) | async-done | bytes 98336 | tf_op jit(solution)/shard_map/all_to_all | solution.py:278
  41.1 0.1 fusion.1.got
  41.2 0.4 shard_map.85
  41.5 1.8 %all-gather.1 = f32[96,128]{1,0:T(8,128)S(1)} all-gather(f32[48,128]{1,0:T(8,128)S(1)} %shard_map.85), channel_id=3, replica_groups={{0,16},{32,48},{64,80},{96,112},{128,144},{160,176},{192,208},{224,240}..., dimensions={0}, use_global_device_ids=true | all-gather | bytes 73728 | tf_op jit(solution)/shard_map/all_gather | solution.py:292
  43.4 13.9 %all_to_all.16.got = bf16[16,48,128]{2,1,0:T(8,128)(2,1)S(1)} all-to-all(bf16[16,48,128]{2,1,0:T(8,128)(2,1)S(1)} %shard_map.86), channel_id=1, replica_groups={{0,32,64,96,128,160,192,224,256,288,320,352,384,416,448,480},{16,48,80,..., dimensions={0} | all-to-all | bytes 393216 | tf_op jit(solution)/shard_map/all_to_all | solution.py:294
  57.3 0.0 copy-done.1
  57.3 0.0 copy-done.2
  57.3 0.9 %shard_map.87 = f32[3,31,128]{2,1,0:T(8,128)} custom-call(f32[32,2,128]{2,1,0:T(2,128)S(1)} %copy-done.2, bf16[16,48,128]{2,1,0:T(8,128)(2,1)S(1)} %all_to_all.16.got, f32[128,256]{1,0:T(8,128)S(1)} %copy-done.1), custom_call_target="tpu_custom_call" | custom-call | tf_op jit(solution)/shard_map/pallas_call | solution.py:243
  (4 shorter events, 0.1 us)
Async XLA Ops:
  0.0 36.8 %copy-start.3 = (f32[48,6]{0,1:T(8,128)S(1)}, f32[48,6]{0,1:T(8,128)}, u32[]{:S(2)}) copy-start(f32[48,6]{0,1:T(8,128)} %param.11) | copy-start | bytes 3460
  28.6 12.5 %all-to-all-start.1 = ((f16[16,24,128]{2,1,0:T(8,128)(2,1)}), f16[16,24,128]{2,1,0:T(8,128)(2,1)S(1)}, u32[]{:S(2)}, u32[]{:S(2)}) async-start(f16[16,24,128]{2,1,0:T(8,128)(2,1)} %broadcast_in_dim.2), calls=%async_computation.1 | async-start | bytes 196608 | tf_op jit(solution)/shard_map/all_to_all | solution.py:278
  36.9 2.0 %copy-start = (bf16[6,2,3,31,1536]{4,1,3,2,0:T(2,128)(2,1)S(1)}, bf16[6,2,3,31,1536]{4,1,3,2,0:T(2,128)(2,1)}, u32[]{:S(2)}) copy-start(bf16[6,2,3,31,1536]{4,1,3,2,0:T(2,128)(2,1)} %param.12) | copy-start | bytes 10285060
  38.8 18.4 %copy-start.1 = (f32[128,256]{1,0:T(8,128)S(1)}, f32[128,256]{1,0:T(8,128)}, u32[]{:S(2)}) copy-start(f32[128,256]{1,0:T(8,128)} %constant.13.clone.table) | copy-start | bytes 393220
  38.8 18.4 %copy-start.2 = (f32[32,2,128]{2,1,0:T(2,128)S(1)}, f32[32,2,128]{2,1,0:T(2,128)}, u32[]{:S(2)}) copy-start(f32[32,2,128]{2,1,0:T(2,128)} %constant.12.clone.turn) | copy-start | bytes 98308

commit v6 on v5

--- a/solution.py
+++ b/solution.py
@@ -273,12 +273,6 @@
     blocks = lax.all_to_all(
         blocks, "patch", 0, 0, axis_index_groups=SAME_CORE, tiled=True
     )
-    code = jnp.sum(blocks.astype(f32), axis=0).astype(f16)
-    codes = jnp.broadcast_to(code[None], (WINDOWS, 24, 128))
-    codes = lax.all_to_all(
-        codes, "freq", 0, 0, axis_index_groups=WINDOW_GROUP, tiled=True
-    )
-    spectra = jnp.sum(decode(codes.astype(f32)), axis=0)
     green = green.transpose(0, 2, 3, 1, 4).reshape(6 * 3 * STA_DEV, 2, OWN * BINS)
     tiles = call(
         moment_kernel,
@@ -288,6 +282,13 @@
         moments.T,
         scratch=[pltpu.VMEM((6, 2, OWN * BINS), f32)],
     )
+    code = jnp.sum(blocks.astype(f32), axis=0).astype(f16)
+    code, tiles = lax.optimization_barrier((code, tiles))
+    codes = jnp.broadcast_to(code[None], (WINDOWS, 24, 128))
+    codes = lax.all_to_all(
+        codes, "freq", 0, 0, axis_index_groups=WINDOW_GROUP, tiled=True
+    )
+    spectra = jnp.sum(decode(codes.astype(f32)), axis=0)
     partial = call(patch_kernel, (48, 128), [VMEM, VMEM], tiles, spectra)
     pair = lax.all_gather(partial, "patch", axis_index_groups=CORE_PAIRS)
     copies = call(spread_half_kernel, (16, 48, 128), [VMEM], pair, dtype=bf16)

time: 58.5 us -> 57.8 us (0.988)
  blocking collectives: 40.5 us -> 29.4 us
  waiting for transfers between devices: 1.22 us -> 7 us
  starting transfers between devices: 8.2 us -> 12.9 us
  other arithmetic: 0.1 us -> 0.73 us
  local copies, waits for them, and re-layouts: 2.63 us -> 2 us
    all_to_all x1, blocking collectives: 22.7 us -> 12 us  [local(): lax.all_to_all(codes, 'freq', 0, 0, axis_index_groups=WINDOW_GROUP, tiled...]
    all_to_all x1, waiting for transfers between devices: 1.22 us -> 7 us  [local(): lax.all_to_all(blocks, 'patch', 0, 0, axis_index_groups=SAME_CORE, tiled=...]
    all_to_all x1, starting transfers between devices: 8.2 us -> 12.9 us  [local(): lax.all_to_all(blocks, 'patch', 0, 0, axis_index_groups=SAME_CORE, tiled=...]
    convert_element_type x1, other arithmetic: 0.02 us -> 0.65 us  [local(): blocks = call(route_kernel, (16, 24, 128), [VMEM], held).astype(f16)]
    broadcast_in_dim x1, local copies, waits for them, and re-layouts: 0.65 us -> 0.02 us  [local(): codes = jnp.broadcast_to(code[None], (WINDOWS, 24, 128))]
where the time goes in v6:
time: 57.8 us; the launch traced here: 57.4 us
  blocking collectives  29.4 us (51%)
  starting transfers between devices  12.9 us (22%)
  waiting for transfers between devices  7 us (12%)
  Pallas kernels  4.69 us (8%)
  local copies, waits for them, and re-layouts  2 us (3%)
  between operations  0.76 us (1%)
  other arithmetic  0.73 us (1%)
    all_to_all x1, blocking collectives, local(): lax.all_to_all(copies, 'patch', 0, 0, axis_index_groups=SAME_CORE, tiled=...  13.5 us
    all_to_all x1, starting transfers between devices, local(): lax.all_to_all(blocks, 'patch', 0, 0, axis_index_groups=SAME_CORE, tiled=...  12.9 us
    all_to_all x1, blocking collectives, local(): lax.all_to_all(codes, 'freq', 0, 0, axis_index_groups=WINDOW_GROUP, tiled...  12 us
    all_to_all x1, waiting for transfers between devices, local(): lax.all_to_all(blocks, 'patch', 0, 0, axis_index_groups=SAME_CORE, tiled=...  7 us
    pallas_call x6, Pallas kernels, call(): pl.pallas_call(kernel, out_shape=jax.ShapeDtypeStruct(shape, dtype), in_s...  4.69 us
    all_gather x1, blocking collectives, local(): held = lax.all_gather(held, 'patch', axis_index_groups=CORE_PAIRS)  2.09 us
    unnamed x8, local copies, waits for them, and re-layouts  1.98 us
    all_gather x1, blocking collectives, local(): pair = lax.all_gather(partial, 'patch', axis_index_groups=CORE_PAIRS)  1.85 us
  transfers between devices with their start and end apart: 1, of which 1 were waited for; matrix products, arithmetic and copies ran while one was open for 0% of the time, Pallas kernels for 2%

profile of v6, /device:TPU:8, one launch (start us, length us, event | category | flops | bytes accessed | tf_op | source)
XLA Modules:
  0.0 57.4 jit_solution(12526788868351108263)
XLA Ops:
  0.0 0.0 copy-start.3
  0.7 1.8 %shard_map.82 = f32[96,128]{1,0:T(8,128)} custom-call(s32[1,1]{1,0:T(1,128)} %bitcast.8.count_hbm, bf16[84,256]{1,0:T(8,128)(2,1)} %slip_hbm.1, s32[1,84]{1,0:T(1,128)} %bitcast.13, f32[16,256,128]{2,1,0:T(8,128)} %constant.4.clone.table_hbm), custom_call_target="tpu_custom_call" | custom-call | tf_op jit(solution)/shard_map/pallas_call | solution.py:243
  2.4 2.1 %all-gather = f32[192,128]{1,0:T(8,128)S(1)} all-gather(f32[96,128]{1,0:T(8,128)} %shard_map.82), channel_id=2, replica_groups={{0,16},{32,48},{64,80},{96,112},{128,144},{160,176},{192,208},{224,240}..., dimensions={0}, use_global_device_ids=true | all-gather | bytes 147456 | tf_op jit(solution)/shard_map/all_gather | solution.py:271
  4.5 0.7 %shard_map.83 = f32[16,24,128]{2,1,0:T(8,128)S(1)} custom-call(f32[2,96,128]{2,1,0:T(8,128)S(1)} %bitcast.10), custom_call_target="tpu_custom_call" | custom-call | tf_op jit(solution)/shard_map/pallas_call | solution.py:243
  5.2 0.7 %convert_element_type.12 = f16[16,24,128]{2,1,0:T(8,128)(2,1)} convert(f32[16,24,128]{2,1,0:T(8,128)S(1)} %shard_map.83) | non-fusion elementwise | flops 49152 | bytes 294912 | tf_op jit(solution)/shard_map/convert_element_type | solution.py:272
  5.9 12.9 %all-to-all-start = ((f16[16,24,128]{2,1,0:T(8,128)(2,1)}), f16[16,24,128]{2,1,0:T(8,128)(2,1)S(1)}, u32[]{:S(2)}, u32[]{:S(2)}) async-start(f16[16,24,128]{2,1,0:T(8,128)(2,1)} %convert_element_type.12), calls=%async_computation | async-start | bytes 196608 | tf_op jit(solution)/shard_map/all_to_all | solution.py:273
  18.7 0.0 copy-done.3
  18.7 0.0 copy-start
  18.8 2.0 %copy-done = bf16[6,2,3,31,1536]{4,1,3,2,0:T(2,128)(2,1)S(1)} copy-done((bf16[6,2,3,31,1536]{4,1,3,2,0:T(2,128)(2,1)S(1)}, bf16[6,2,3,31,1536]{4,1,3,2,0:T(2,128)(2,1)}, u32[]{:S(2)}) %copy-start) | copy-done | bytes 3428376
  20.7 1.0 %shard_map.84.tiles = f32[93,24,128]{2,1,0:T(8,128)S(1)} custom-call(bf16[558,2,1536]{2,1,0:T(2,128)(2,1)S(1)} %bitcast.9, f32[6,48]{1,0:T(8,128)S(1)} %bitcast.12), custom_call_target="tpu_custom_call" | custom-call | tf_op jit(solution)/shard_map/pallas_call | solution.py:243
  21.8 0.0 copy-start.1
  21.8 0.0 copy-start.2
  21.8 7.0 %all-to-all-done = f16[16,24,128]{2,1,0:T(8,128)(2,1)S(1)} async-done(((f16[16,24,128]{2,1,0:T(8,128)(2,1)}), f16[16,24,128]{2,1,0:T(8,128)(2,1)S(1)}, u32[]{:S(2)}, u32[]{:S(2)}) %all-to-all-start) | async-done | bytes 98336 | tf_op jit(solution)/shard_map/all_to_all | solution.py:273
  28.8 12.0 %all_to_all.15 = f16[16,24,128]{2,1,0:T(8,128)(2,1)S(1)} all-to-all(f16[16,24,128]{2,1,0:T(8,128)(2,1)S(1)} %broadcast_in_dim.2), channel_id=1, replica_groups={{9,7,5,3,1,15,13,11,8,6,4,2,0,14,12,10},{25,23,21,19,17,31,29,27,24,22,..., dimensions={0} | all-to-all | bytes 196608 | tf_op jit(solution)/shard_map/all_to_all | solution.py:288
  40.8 0.1 fusion.1.got
  40.9 0.4 shard_map.85
  41.2 1.8 %all-gather.1 = f32[96,128]{1,0:T(8,128)S(1)} all-gather(f32[48,128]{1,0:T(8,128)S(1)} %shard_map.85), channel_id=3, replica_groups={{0,16},{32,48},{64,80},{96,112},{128,144},{160,176},{192,208},{224,240}..., dimensions={0}, use_global_device_ids=true | all-gather | bytes 73728 | tf_op jit(solution)/shard_map/all_gather | solution.py:293
  43.1 13.5 %all_to_all.16.got = bf16[16,48,128]{2,1,0:T(8,128)(2,1)S(1)} all-to-all(bf16[16,48,128]{2,1,0:T(8,128)(2,1)S(1)} %shard_map.86), channel_id=1, replica_groups={{0,32,64,96,128,160,192,224,256,288,320,352,384,416,448,480},{16,48,80,..., dimensions={0} | all-to-all | bytes 393216 | tf_op jit(solution)/shard_map/all_to_all | solution.py:295
  56.6 0.0 copy-done.1
  56.6 0.0 copy-done.2
  56.6 0.9 %shard_map.87 = f32[3,31,128]{2,1,0:T(8,128)} custom-call(f32[32,2,128]{2,1,0:T(2,128)S(1)} %copy-done.2, bf16[16,48,128]{2,1,0:T(8,128)(2,1)S(1)} %all_to_all.16.got, f32[128,256]{1,0:T(8,128)S(1)} %copy-done.1), custom_call_target="tpu_custom_call" | custom-call | tf_op jit(solution)/shard_map/pallas_call | solution.py:243
  (4 shorter events, 0.1 us)
Async XLA Ops:
  0.0 18.7 %copy-start.3 = (f32[48,6]{0,1:T(8,128)S(1)}, f32[48,6]{0,1:T(8,128)}, u32[]{:S(2)}) copy-start(f32[48,6]{0,1:T(8,128)} %param.11) | copy-start | bytes 3460
  5.9 22.9 %all-to-all-start = ((f16[16,24,128]{2,1,0:T(8,128)(2,1)}), f16[16,24,128]{2,1,0:T(8,128)(2,1)S(1)}, u32[]{:S(2)}, u32[]{:S(2)}) async-start(f16[16,24,128]{2,1,0:T(8,128)(2,1)} %convert_element_type.12), calls=%async_computation | async-start | bytes 196608 | tf_op jit(solution)/shard_map/all_to_all | solution.py:273
  18.7 2.0 %copy-start = (bf16[6,2,3,31,1536]{4,1,3,2,0:T(2,128)(2,1)S(1)}, bf16[6,2,3,31,1536]{4,1,3,2,0:T(2,128)(2,1)}, u32[]{:S(2)}) copy-start(bf16[6,2,3,31,1536]{4,1,3,2,0:T(2,128)(2,1)} %param.12) | copy-start | bytes 10285060
  21.8 34.8 %copy-start.1 = (f32[128,256]{1,0:T(8,128)S(1)}, f32[128,256]{1,0:T(8,128)}, u32[]{:S(2)}) copy-start(f32[128,256]{1,0:T(8,128)} %constant.13.clone.table) | copy-start | bytes 393220
  21.8 34.8 %copy-start.2 = (f32[32,2,128]{2,1,0:T(2,128)S(1)}, f32[32,2,128]{2,1,0:T(2,128)}, u32[]{:S(2)}) copy-start(f32[32,2,128]{2,1,0:T(2,128)} %constant.12.clone.turn) | copy-start | bytes 98308

commit v7 on v6

--- a/solution.py
+++ b/solution.py
@@ -83,24 +83,24 @@
     return jnp.where(code < 0.0, -square, square) * square * (1.0 / CODE_SCALE)
 
 
-def window_kernel(count_hbm, slip_hbm, ids_hbm, table_hbm, out, count, slip, ids, table, sems):
+def window_kernel(count, slip_hbm, ids_hbm, table_hbm, out, slip, ids, table, sems):
     q = lax.axis_index("freq")
     copies = [
         pltpu.make_async_copy(table_hbm.at[q], table, sems.at[0]),
         pltpu.make_async_copy(slip_hbm, slip, sems.at[1]),
         pltpu.make_async_copy(ids_hbm, ids, sems.at[2]),
-        pltpu.make_async_copy(count_hbm, count, sems.at[3]),
     ]
     for copy in copies:
         copy.start()
     out[CAP:ID_ROW, :] = jnp.zeros((ID_ROW - CAP, 128), f32)
     out[ID_ROW:HOLD, :] = jnp.full((HOLD - ID_ROW, 128), -1.0, f32)
-    for copy in copies:
-        copy.wait()
+    copies[0].wait()
     both = jnp.concatenate(split2(table[...]), axis=1)
+    copies[1].wait()
     r = jnp.dot(slip[...], both, preferred_element_type=f32)
     out[0:CAP, :] = encode(r[:, :128] + r[:, 128:])
-    live = lanes((1, CAP)) < count[...]
+    copies[2].wait()
+    live = lanes((1, CAP)) < count[0]
     out[ID_ROW : ID_ROW + 1, 0:CAP] = jnp.where(live, ids[...].astype(f32), -1.0)
 
 
@@ -254,17 +254,16 @@
     held = call(
         window_kernel,
         (HOLD, 128),
-        [HBM] * 4,
-        face_counts.reshape(1, 1),
+        [SMEM] + [HBM] * 3,
+        face_counts,
         slip_rate,
         patch_ids.reshape(1, CAP),
         jnp.asarray(analysis_table()),
         scratch=[
-            pltpu.VMEM((1, 1), jnp.int32),
             pltpu.VMEM((CAP, T // WINDOWS), bf16),
             pltpu.VMEM((1, CAP), jnp.int32),
             pltpu.VMEM((T // WINDOWS, 128), f32),
-            pltpu.SemaphoreType.DMA((4,)),
+            pltpu.SemaphoreType.DMA((3,)),
         ],
         grant=60,
     )

time: 57.8 us -> 57.8 us (level)
  no operation moved by 1% of the time
where the time goes in v7:
time: 57.8 us; the launch traced here: 57.4 us
  blocking collectives  29.4 us (51%)
  starting transfers between devices  12.9 us (22%)
  waiting for transfers between devices  7 us (12%)
  Pallas kernels  4.69 us (8%)
  local copies, waits for them, and re-layouts  2 us (3%)
  between operations  0.76 us (1%)
  other arithmetic  0.73 us (1%)
    all_to_all x1, blocking collectives, local(): lax.all_to_all(copies, 'patch', 0, 0, axis_index_groups=SAME_CORE, tiled=...  13.5 us
    all_to_all x1, starting transfers between devices, local(): lax.all_to_all(blocks, 'patch', 0, 0, axis_index_groups=SAME_CORE, tiled=...  12.9 us
    all_to_all x1, blocking collectives, local(): lax.all_to_all(codes, 'freq', 0, 0, axis_index_groups=WINDOW_GROUP, tiled...  12 us
    all_to_all x1, waiting for transfers between devices, local(): lax.all_to_all(blocks, 'patch', 0, 0, axis_index_groups=SAME_CORE, tiled=...  7 us
    pallas_call x6, Pallas kernels, call(): pl.pallas_call(kernel, out_shape=jax.ShapeDtypeStruct(shape, dtype), in_s...  4.69 us
    all_gather x1, blocking collectives, local(): held = lax.all_gather(held, 'patch', axis_index_groups=CORE_PAIRS)  2.09 us
    unnamed x8, local copies, waits for them, and re-layouts  1.98 us
    all_gather x1, blocking collectives, local(): pair = lax.all_gather(partial, 'patch', axis_index_groups=CORE_PAIRS)  1.85 us
  transfers between devices with their start and end apart: 1, of which 1 were waited for; matrix products, arithmetic and copies ran while one was open for 0% of the time, Pallas kernels for 2%

profile of v7, /device:TPU:8, one launch (start us, length us, event | category | flops | bytes accessed | tf_op | source)
XLA Modules:
  0.0 57.4 jit_solution(17940786200826926771)
XLA Ops:
  0.0 0.0 copy-start.3
  0.7 1.8 %shard_map.82 = f32[96,128]{1,0:T(8,128)} custom-call(s32[1]{0:T(128)S(6)} %copy.9.count, bf16[84,256]{1,0:T(8,128)(2,1)} %slip_hbm.1, s32[1,84]{1,0:T(1,128)} %bitcast.11, f32[16,256,128]{2,1,0:T(8,128)} %constant.4.clone.table_hbm), custom_call_target="tpu_custom_call" | custom-call | tf_op jit(solution)/shard_map/pallas_call | solution.py:243
  2.4 2.1 %all-gather = f32[192,128]{1,0:T(8,128)S(1)} all-gather(f32[96,128]{1,0:T(8,128)} %shard_map.82), channel_id=2, replica_groups={{0,16},{32,48},{64,80},{96,112},{128,144},{160,176},{192,208},{224,240}..., dimensions={0}, use_global_device_ids=true | all-gather | bytes 147456 | tf_op jit(solution)/shard_map/all_gather | solution.py:270
  4.5 0.7 %shard_map.83 = f32[16,24,128]{2,1,0:T(8,128)S(1)} custom-call(f32[2,96,128]{2,1,0:T(8,128)S(1)} %bitcast.8), custom_call_target="tpu_custom_call" | custom-call | tf_op jit(solution)/shard_map/pallas_call | solution.py:243
  5.2 0.7 %convert_element_type.12 = f16[16,24,128]{2,1,0:T(8,128)(2,1)} convert(f32[16,24,128]{2,1,0:T(8,128)S(1)} %shard_map.83) | non-fusion elementwise | flops 49152 | bytes 294912 | tf_op jit(solution)/shard_map/convert_element_type | solution.py:271
  5.9 12.9 %all-to-all-start = ((f16[16,24,128]{2,1,0:T(8,128)(2,1)}), f16[16,24,128]{2,1,0:T(8,128)(2,1)S(1)}, u32[]{:S(2)}, u32[]{:S(2)}) async-start(f16[16,24,128]{2,1,0:T(8,128)(2,1)} %convert_element_type.12), calls=%async_computation | async-start | bytes 196608 | tf_op jit(solution)/shard_map/all_to_all | solution.py:272
  18.7 0.0 copy-done.3
  18.7 0.0 copy-start
  18.8 2.0 %copy-done = bf16[6,2,3,31,1536]{4,1,3,2,0:T(2,128)(2,1)S(1)} copy-done((bf16[6,2,3,31,1536]{4,1,3,2,0:T(2,128)(2,1)S(1)}, bf16[6,2,3,31,1536]{4,1,3,2,0:T(2,128)(2,1)}, u32[]{:S(2)}) %copy-start) | copy-done | bytes 3428376
  20.7 1.0 %shard_map.84.tiles = f32[93,24,128]{2,1,0:T(8,128)S(1)} custom-call(bf16[558,2,1536]{2,1,0:T(2,128)(2,1)S(1)} %bitcast.7, f32[6,48]{1,0:T(8,128)S(1)} %bitcast.10), custom_call_target="tpu_custom_call" | custom-call | tf_op jit(solution)/shard_map/pallas_call | solution.py:243
  21.8 0.0 copy-start.1
  21.8 0.0 copy-start.2
  21.8 7.0 %all-to-all-done = f16[16,24,128]{2,1,0:T(8,128)(2,1)S(1)} async-done(((f16[16,24,128]{2,1,0:T(8,128)(2,1)}), f16[16,24,128]{2,1,0:T(8,128)(2,1)S(1)}, u32[]{:S(2)}, u32[]{:S(2)}) %all-to-all-start) | async-done | bytes 98336 | tf_op jit(solution)/shard_map/all_to_all | solution.py:272
  28.8 12.0 %all_to_all.15 = f16[16,24,128]{2,1,0:T(8,128)(2,1)S(1)} all-to-all(f16[16,24,128]{2,1,0:T(8,128)(2,1)S(1)} %broadcast_in_dim.2), channel_id=1, replica_groups={{9,7,5,3,1,15,13,11,8,6,4,2,0,14,12,10},{25,23,21,19,17,31,29,27,24,22,..., dimensions={0} | all-to-all | bytes 196608 | tf_op jit(solution)/shard_map/all_to_all | solution.py:287
  40.8 0.1 fusion.1.got
  40.9 0.4 shard_map.85
  41.2 1.8 %all-gather.1 = f32[96,128]{1,0:T(8,128)S(1)} all-gather(f32[48,128]{1,0:T(8,128)S(1)} %shard_map.85), channel_id=3, replica_groups={{0,16},{32,48},{64,80},{96,112},{128,144},{160,176},{192,208},{224,240}..., dimensions={0}, use_global_device_ids=true | all-gather | bytes 73728 | tf_op jit(solution)/shard_map/all_gather | solution.py:292
  43.1 13.5 %all_to_all.16.got = bf16[16,48,128]{2,1,0:T(8,128)(2,1)S(1)} all-to-all(bf16[16,48,128]{2,1,0:T(8,128)(2,1)S(1)} %shard_map.86), channel_id=1, replica_groups={{0,32,64,96,128,160,192,224,256,288,320,352,384,416,448,480},{16,48,80,..., dimensions={0} | all-to-all | bytes 393216 | tf_op jit(solution)/shard_map/all_to_all | solution.py:294
  56.6 0.0 copy-done.1
  56.6 0.0 copy-done.2
  56.6 0.9 %shard_map.87 = f32[3,31,128]{2,1,0:T(8,128)} custom-call(f32[32,2,128]{2,1,0:T(2,128)S(1)} %copy-done.2, bf16[16,48,128]{2,1,0:T(8,128)(2,1)S(1)} %all_to_all.16.got, f32[128,256]{1,0:T(8,128)S(1)} %copy-done.1), custom_call_target="tpu_custom_call" | custom-call | tf_op jit(solution)/shard_map/pallas_call | solution.py:243
  (4 shorter events, 0.1 us)
Async XLA Ops:
  0.0 18.7 %copy-start.3 = (f32[48,6]{0,1:T(8,128)S(1)}, f32[48,6]{0,1:T(8,128)}, u32[]{:S(2)}) copy-start(f32[48,6]{0,1:T(8,128)} %param.11) | copy-start | bytes 3460
  5.9 22.9 %all-to-all-start = ((f16[16,24,128]{2,1,0:T(8,128)(2,1)}), f16[16,24,128]{2,1,0:T(8,128)(2,1)S(1)}, u32[]{:S(2)}, u32[]{:S(2)}) async-start(f16[16,24,128]{2,1,0:T(8,128)(2,1)} %convert_element_type.12), calls=%async_computation | async-start | bytes 196608 | tf_op jit(solution)/shard_map/all_to_all | solution.py:272
  18.7 2.0 %copy-start = (bf16[6,2,3,31,1536]{4,1,3,2,0:T(2,128)(2,1)S(1)}, bf16[6,2,3,31,1536]{4,1,3,2,0:T(2,128)(2,1)}, u32[]{:S(2)}) copy-start(bf16[6,2,3,31,1536]{4,1,3,2,0:T(2,128)(2,1)} %param.12) | copy-start | bytes 10285060
  21.8 34.8 %copy-start.1 = (f32[128,256]{1,0:T(8,128)S(1)}, f32[128,256]{1,0:T(8,128)}, u32[]{:S(2)}) copy-start(f32[128,256]{1,0:T(8,128)} %constant.13.clone.table) | copy-start | bytes 393220
  21.8 34.8 %copy-start.2 = (f32[32,2,128]{2,1,0:T(2,128)S(1)}, f32[32,2,128]{2,1,0:T(2,128)}, u32[]{:S(2)}) copy-start(f32[32,2,128]{2,1,0:T(2,128)} %constant.12.clone.turn) | copy-start | bytes 98308

commit v8 on v6

--- a/solution.py
+++ b/solution.py
@@ -20,6 +20,9 @@
 ID_ROW = 88
 
 CORE_PAIRS = [[2 * d, 2 * d + 1] for d in range(16)]
+FROM_TOP = [
+    [16 * x + 2 * ((z + 7) % 8) + c for x in range(2) for z in range(8)] for c in range(2)
+]
 SAME_CORE = [[2 * d + c for d in range(16)] for c in range(2)]
 DOWN_Y = [4, 3, 2, 1, 0, 7, 6, 5]
 WINDOW_GROUP = [[2 * y + x for x in (1, 0) for y in DOWN_Y]]
@@ -110,7 +113,8 @@
     r = rows((n, 128))
     d = lax.shift_right_logical(r * 2731, 16)
     j = lax.shift_right_logical(r - 24 * d, 1)
-    base = (96 * d + 4 * j).astype(f32)
+    place = 8 * lax.shift_right_logical(d, 3) + ((d + 7) & 7)
+    base = (96 * place + 4 * j).astype(f32)
     base = base + 48.0 * core
     block = lax.shift_right_logical(lanes((HOLD, 256)), 5) % 4
     odd = lax.rem(lax.shift_right_logical(lanes((HOLD, 128)), 5), 2) == 1
@@ -271,7 +275,7 @@
     held = lax.all_gather(held, "patch", axis_index_groups=CORE_PAIRS)
     blocks = call(route_kernel, (16, 24, 128), [VMEM], held).astype(f16)
     blocks = lax.all_to_all(
-        blocks, "patch", 0, 0, axis_index_groups=SAME_CORE, tiled=True
+        blocks, "patch", 0, 0, axis_index_groups=FROM_TOP, tiled=True
     )
     green = green.transpose(0, 2, 3, 1, 4).reshape(6 * 3 * STA_DEV, 2, OWN * BINS)
     tiles = call(

time: 57.8 us -> 58 us (level)
  waiting for transfers between devices: 7 us -> 4.96 us
  blocking collectives: 29.4 us -> 31.2 us
    all_to_all x1, waiting for transfers between devices: 7 us -> 4.96 us  [local(): lax.all_to_all(blocks, 'patch', 0, 0, axis_index_groups=FROM_TOP, tiled=T...]
    all_to_all x1, blocking collectives: 13.5 us -> 15.2 us  [local(): lax.all_to_all(copies, 'patch', 0, 0, axis_index_groups=SAME_CORE, tiled=...]
where the time goes in v8:
time: 58 us; the launch traced here: 57.6 us
  blocking collectives  31.2 us (54%)
  starting transfers between devices  13.3 us (23%)
  waiting for transfers between devices  4.96 us (9%)
  Pallas kernels  4.7 us (8%)
  local copies, waits for them, and re-layouts  2 us (3%)
  between operations  0.74 us (1%)
  other arithmetic  0.73 us (1%)
    all_to_all x1, blocking collectives, local(): lax.all_to_all(copies, 'patch', 0, 0, axis_index_groups=SAME_CORE, tiled=...  15.2 us
    all_to_all x1, starting transfers between devices, local(): lax.all_to_all(blocks, 'patch', 0, 0, axis_index_groups=FROM_TOP, tiled=T...  13.3 us
    all_to_all x1, blocking collectives, local(): lax.all_to_all(codes, 'freq', 0, 0, axis_index_groups=WINDOW_GROUP, tiled...  12 us
    all_to_all x1, waiting for transfers between devices, local(): lax.all_to_all(blocks, 'patch', 0, 0, axis_index_groups=FROM_TOP, tiled=T...  4.96 us
    pallas_call x6, Pallas kernels, call(): pl.pallas_call(kernel, out_shape=jax.ShapeDtypeStruct(shape, dtype), in_s...  4.7 us
    all_gather x1, blocking collectives, local(): held = lax.all_gather(held, 'patch', axis_index_groups=CORE_PAIRS)  2.09 us
    unnamed x8, local copies, waits for them, and re-layouts  1.98 us
    all_gather x1, blocking collectives, local(): pair = lax.all_gather(partial, 'patch', axis_index_groups=CORE_PAIRS)  1.85 us
  transfers between devices with their start and end apart: 1, of which 1 were waited for; matrix products, arithmetic and copies ran while one was open for 0% of the time, Pallas kernels for 2%

profile of v8, /device:TPU:8, one launch (start us, length us, event | category | flops | bytes accessed | tf_op | source)
XLA Modules:
  0.0 57.6 jit_solution(7715857477556568349)
XLA Ops:
  0.0 0.0 copy-start.3
  0.7 1.8 %shard_map.82 = f32[96,128]{1,0:T(8,128)} custom-call(s32[1,1]{1,0:T(1,128)} %bitcast.8.count_hbm, bf16[84,256]{1,0:T(8,128)(2,1)} %slip_hbm.1, s32[1,84]{1,0:T(1,128)} %bitcast.13, f32[16,256,128]{2,1,0:T(8,128)} %constant.4.clone.table_hbm), custom_call_target="tpu_custom_call" | custom-call | tf_op jit(solution)/shard_map/pallas_call | solution.py:247
  2.4 2.1 %all-gather = f32[192,128]{1,0:T(8,128)S(1)} all-gather(f32[96,128]{1,0:T(8,128)} %shard_map.82), channel_id=2, replica_groups={{0,16},{32,48},{64,80},{96,112},{128,144},{160,176},{192,208},{224,240}..., dimensions={0}, use_global_device_ids=true | all-gather | bytes 147456 | tf_op jit(solution)/shard_map/all_gather | solution.py:275
  4.5 0.7 %shard_map.83 = f32[16,24,128]{2,1,0:T(8,128)S(1)} custom-call(f32[2,96,128]{2,1,0:T(8,128)S(1)} %bitcast.10), custom_call_target="tpu_custom_call" | custom-call | tf_op jit(solution)/shard_map/pallas_call | solution.py:247
  5.2 0.7 %convert_element_type.12 = f16[16,24,128]{2,1,0:T(8,128)(2,1)} convert(f32[16,24,128]{2,1,0:T(8,128)S(1)} %shard_map.83) | non-fusion elementwise | flops 49152 | bytes 294912 | tf_op jit(solution)/shard_map/convert_element_type | solution.py:276
  5.9 13.3 %all-to-all-start = ((f16[16,24,128]{2,1,0:T(8,128)(2,1)}), f16[16,24,128]{2,1,0:T(8,128)(2,1)S(1)}, u32[]{:S(2)}, u32[]{:S(2)}) async-start(f16[16,24,128]{2,1,0:T(8,128)(2,1)} %convert_element_type.12), calls=%async_computation | async-start | bytes 196608 | tf_op jit(solution)/shard_map/all_to_all | solution.py:277
  19.2 0.0 copy-done.3
  19.2 0.0 copy-start
  19.2 2.0 %copy-done = bf16[6,2,3,31,1536]{4,1,3,2,0:T(2,128)(2,1)S(1)} copy-done((bf16[6,2,3,31,1536]{4,1,3,2,0:T(2,128)(2,1)S(1)}, bf16[6,2,3,31,1536]{4,1,3,2,0:T(2,128)(2,1)}, u32[]{:S(2)}) %copy-start) | copy-done | bytes 3428376
  21.2 1.0 %shard_map.84.tiles = f32[93,24,128]{2,1,0:T(8,128)S(1)} custom-call(bf16[558,2,1536]{2,1,0:T(2,128)(2,1)S(1)} %bitcast.9, f32[6,48]{1,0:T(8,128)S(1)} %bitcast.12), custom_call_target="tpu_custom_call" | custom-call | tf_op jit(solution)/shard_map/pallas_call | solution.py:247
  22.2 0.0 copy-start.1
  22.2 0.0 copy-start.2
  22.3 5.0 %all-to-all-done = f16[16,24,128]{2,1,0:T(8,128)(2,1)S(1)} async-done(((f16[16,24,128]{2,1,0:T(8,128)(2,1)}), f16[16,24,128]{2,1,0:T(8,128)(2,1)S(1)}, u32[]{:S(2)}, u32[]{:S(2)}) %all-to-all-start) | async-done | bytes 98336 | tf_op jit(solution)/shard_map/all_to_all | solution.py:277
  27.3 12.0 %all_to_all.15 = f16[16,24,128]{2,1,0:T(8,128)(2,1)S(1)} all-to-all(f16[16,24,128]{2,1,0:T(8,128)(2,1)S(1)} %broadcast_in_dim.2), channel_id=1, replica_groups={{9,7,5,3,1,15,13,11,8,6,4,2,0,14,12,10},{25,23,21,19,17,31,29,27,24,22,..., dimensions={0} | all-to-all | bytes 196608 | tf_op jit(solution)/shard_map/all_to_all | solution.py:292
  39.2 0.1 fusion.1.got
  39.3 0.4 shard_map.85
  39.7 1.8 %all-gather.1 = f32[96,128]{1,0:T(8,128)S(1)} all-gather(f32[48,128]{1,0:T(8,128)S(1)} %shard_map.85), channel_id=3, replica_groups={{0,16},{32,48},{64,80},{96,112},{128,144},{160,176},{192,208},{224,240}..., dimensions={0}, use_global_device_ids=true | all-gather | bytes 73728 | tf_op jit(solution)/shard_map/all_gather | solution.py:297
  41.5 15.2 %all_to_all.16.got = bf16[16,48,128]{2,1,0:T(8,128)(2,1)S(1)} all-to-all(bf16[16,48,128]{2,1,0:T(8,128)(2,1)S(1)} %shard_map.86), channel_id=1, replica_groups={{0,32,64,96,128,160,192,224,256,288,320,352,384,416,448,480},{16,48,80,..., dimensions={0} | all-to-all | bytes 393216 | tf_op jit(solution)/shard_map/all_to_all | solution.py:299
  56.8 0.0 copy-done.1
  56.8 0.0 copy-done.2
  56.8 0.9 %shard_map.87 = f32[3,31,128]{2,1,0:T(8,128)} custom-call(f32[32,2,128]{2,1,0:T(2,128)S(1)} %copy-done.2, bf16[16,48,128]{2,1,0:T(8,128)(2,1)S(1)} %all_to_all.16.got, f32[128,256]{1,0:T(8,128)S(1)} %copy-done.1), custom_call_target="tpu_custom_call" | custom-call | tf_op jit(solution)/shard_map/pallas_call | solution.py:247
  (4 shorter events, 0.1 us)
Async XLA Ops:
  0.0 19.2 %copy-start.3 = (f32[48,6]{0,1:T(8,128)S(1)}, f32[48,6]{0,1:T(8,128)}, u32[]{:S(2)}) copy-start(f32[48,6]{0,1:T(8,128)} %param.11) | copy-start | bytes 3460
  5.9 21.3 %all-to-all-start = ((f16[16,24,128]{2,1,0:T(8,128)(2,1)}), f16[16,24,128]{2,1,0:T(8,128)(2,1)S(1)}, u32[]{:S(2)}, u32[]{:S(2)}) async-start(f16[16,24,128]{2,1,0:T(8,128)(2,1)} %convert_element_type.12), calls=%async_computation | async-start | bytes 196608 | tf_op jit(solution)/shard_map/all_to_all | solution.py:277
  19.2 2.0 %copy-start = (bf16[6,2,3,31,1536]{4,1,3,2,0:T(2,128)(2,1)S(1)}, bf16[6,2,3,31,1536]{4,1,3,2,0:T(2,128)(2,1)}, u32[]{:S(2)}) copy-start(bf16[6,2,3,31,1536]{4,1,3,2,0:T(2,128)(2,1)} %param.12) | copy-start | bytes 10285060
  22.2 34.5 %copy-start.1 = (f32[128,256]{1,0:T(8,128)S(1)}, f32[128,256]{1,0:T(8,128)}, u32[]{:S(2)}) copy-start(f32[128,256]{1,0:T(8,128)} %constant.13.clone.table) | copy-start | bytes 393220
  22.2 34.5 %copy-start.2 = (f32[32,2,128]{2,1,0:T(2,128)S(1)}, f32[32,2,128]{2,1,0:T(2,128)}, u32[]{:S(2)}) copy-start(f32[32,2,128]{2,1,0:T(2,128)} %constant.12.clone.turn) | copy-start | bytes 98308
